TPU v7x, 256 devices: a whole 4x4x8 slice. The times are simulated.
256 devices in a mesh: band: 32 (over x, z_hi, core), grid: 8 (over y, z_lo).
Axes of the slice: x: 4, y: 4, z: 8 (z_hi: 4, z_lo: 2; z = z_hi * 2 + z_lo), core: 2. Of those that a mesh axis runs over, the one named last changes fastest.
Arguments:
- orbitals: bfloat16 [64, 96, 96, 96], P('band', 'grid'), may hold values from -2 to 2
- exchange_in: float32 [64, 96, 96, 96], P('band', 'grid'), may hold values from -2 to 2
- window_slot: int32 [32], P('band'), may hold values from 0 to 1
- task_pairs: int32 [32, 2, 8], P('band'), may hold values from 0 to 31
- task_count: int32 [32], P('band'), may hold values from 1 to 8, 128 in all
Outputs:
- exchange_out: float32 [64, 96, 96, 96], P('band', 'grid')
Inputs may be any that keep to these rules, and one draw needn't show every extreme that they name: task_pairs[g, 0, k] and task_pairs[g, 1, k] are the window positions of the source and target band of task k of band group g; entries with k >= task_count[g] are ignored. `task_count`: some band group has exactly 8 live tasks.
All inputs are finite; a program needn't handle non-finite values.
Results may differ from a plain program's by a relative error of at most 0.0003.
Values may be sent and summed in bfloat16 or wider, within the bound.
A program may use at most 128 MiB of HBM per device.

v0:
```python
import math

import jax
import jax.numpy as jnp
from jax import lax
from jax.sharding import PartitionSpec as P


def hartley_table(length):
    steps_all = jnp.arange(length, dtype=jnp.int32)
    product = steps_all[:, None] * steps_all[None, :] % length
    angle_table = product.astype(jnp.float32) * (2.0 * math.pi / length)
    return jnp.cos(angle_table) + jnp.sin(angle_table)


def wavenumbers(length):
    steps_all = jnp.arange(length, dtype=jnp.int32)
    signed = jnp.where(steps_all <= length // 2, steps_all, steps_all - length)
    return signed.astype(jnp.float32) * (2.0 * math.pi / length)


def pencil_kernel(span_first, span_second, span_third, slab_second, grid_index):
    wave_first = wavenumbers(span_first)[:, None, None]
    wave_second = lax.dynamic_slice_in_dim(
        wavenumbers(span_second), grid_index * slab_second, slab_second
    )[None, :, None]
    wave_third = wavenumbers(span_third)[None, None, :]
    square = wave_first * wave_first + wave_second * wave_second + wave_third * wave_third
    safe_square = jnp.where(square > 0, square, 1.0)
    factor = 4.0 * math.pi / (span_first * span_second * span_third)
    kernel = jnp.where(square > 0, factor / safe_square, 0.0)
    return kernel.reshape(span_first, slab_second * span_third)


def transform_inner(values_in, table_second, table_third):
    mixed = jnp.einsum("bxyz,zk->bxyk", values_in, table_third, precision=lax.Precision.HIGHEST)
    return jnp.einsum("bxyk,yj->bxjk", mixed, table_second, precision=lax.Precision.HIGHEST)


def on_device(orbitals, exchange_in, window_slot, task_pairs, task_count):
    band_dev, slab_rows, span_second, span_third = orbitals.shape
    grid_parts = lax.axis_size("grid")
    groups = lax.axis_size("band")
    span_first = slab_rows * grid_parts
    slab_second = span_second // grid_parts
    table_first = hartley_table(span_first)
    table_second = hartley_table(span_second)
    table_third = hartley_table(span_third)
    kernel = pencil_kernel(span_first, span_second, span_third, slab_second, lax.axis_index("grid"))
    mine = lax.dynamic_index_in_dim(orbitals, window_slot[0], 0, keepdims=True)
    window = lax.all_gather(mine, "band", axis=0, tiled=True)

    def solve_pencils(pencils):
        batch_size = pencils.shape[0]
        flat = pencils.reshape(batch_size, span_first, slab_second * span_third)
        spectrum = (
            jnp.einsum("bxm,xi->bim", flat, table_first, precision=lax.Precision.HIGHEST) * kernel
        )
        restored = jnp.einsum("bim,ix->bxm", spectrum, table_first, precision=lax.Precision.HIGHEST)
        restored = restored.reshape(batch_size, span_first, 1, slab_second * span_third)
        return lax.all_to_all(restored, "grid", split_axis=1, concat_axis=2, tiled=True)

    def potential_of(density):
        batch_size = density.shape[0]
        mixed = transform_inner(density, table_second, table_third)
        mixed = mixed.reshape(batch_size, slab_rows, grid_parts, slab_second * span_third)
        solved = solve_pencils(
            lax.all_to_all(mixed, "grid", split_axis=2, concat_axis=1, tiled=True)
        )
        solved = solved.reshape(batch_size, slab_rows, span_second, span_third)
        return transform_inner(solved, table_second, table_third)

    def add_terms(partial_value, sources, targets, weights, dest_rows):
        source_orb = jnp.take(window, sources, axis=0).astype(jnp.float32)
        target_orb = jnp.take(window, targets, axis=0).astype(jnp.float32)
        potential = potential_of(source_orb * target_orb)
        contribution = potential * source_orb * weights[:, None, None, None]
        return partial_value.at[dest_rows].add(contribution)

    task_total = task_count[0]

    def fetch(position):
        return (task_pairs[0, 0, position], task_pairs[0, 1, position])

    partial_value = jnp.zeros((groups, slab_rows, span_second, span_third), jnp.float32)

    def step_single(position, partial_now):
        source, target = fetch(position)
        targets = target[None]
        return add_terms(partial_now, source[None], targets, jnp.ones((1,), jnp.float32), targets)

    partial_value = lax.fori_loop(jnp.int32(0), task_total, step_single, partial_value)
    owned = lax.psum_scatter(partial_value, "band", scatter_dimension=0, tiled=True)
    slot_ids = jnp.arange(band_dev, dtype=jnp.int32)[:, None, None, None]
    return exchange_in + jnp.where(slot_ids == window_slot[0], owned, 0.0)


def solution(mesh):
    in_specs = (
        P("band", "grid", None, None),
        P("band", "grid", None, None),
        P("band"),
        P("band", None, None),
        P("band"),
    )
    out_specs = P("band", "grid", None, None)
    return jax.shard_map(
        on_device, mesh=mesh, in_specs=in_specs, out_specs=out_specs, check_vma=False
    )
```

profile of v0, /device:TPU:1, one launch (start us, length us, event | category | flops | bytes accessed | tf_op | source)
XLA Modules:
  0.0 635.6 jit_solution(8970746149572828790)
XLA Ops:
  6.5 0.0 copy-start
  6.5 0.0 all-gather.2.cloned.1.call-start
  7.3 0.4 copy-done
  7.6 0.7 constant_dynamic-slice_fusion.2
  8.3 0.0 all-gather.2.cloned.1.call-update
  8.4 0.0 reduce-scatter.2.cloned.1.call-start
  8.5 0.1 dynamic-slice_multiply_fusion
  8.5 0.1 broadcast_add_fusion
  8.6 89.6 %all-gather.2.cloned.1.call-done = bf16[32,12,96,96]{3,2,1,0:T(8,128)(2,1)} async-done(((bf16[1,12,96,96]{3,2,1,0:T(8,128)(2,1)}), bf16[32,12,96,96]{3,2,1,0:T(8,128)(2,1)}) %all-gather.2.cloned.1.call-update) | async-done | bytes 7077904 | tf_op jit(solution)/shard_map/all_gather | solution.py:51
  98.2 12.6 %copy.52 = bf16[32,12,96,96]{2,3,1,0:T(8,128)(2,1)} copy(bf16[32,12,96,96]{3,2,1,0:T(8,128)(2,1)} %all-gather.2.cloned.1.call-done) | data formatting | bytes 14155776
  110.8 0.0 copy-start.2
  110.8 0.0 copy-start.3
  110.8 8.9 %broadcast_in_dim.52 = f32[32,12,96,96]{2,3,1,0:T(8,128)} broadcast(f32[]{:T(128)} %constant.89.clone.1), dimensions={} | broadcast | bytes 14155780 | tf_op jit(solution)/shard_map/broadcast_in_dim | solution.py:85
  119.7 0.0 copy-done.2
  119.7 0.0 copy-done.3
  119.7 42.8 %while.15 = (s32[]{:T(128)}, f32[32,12,96,96]{2,3,1,0:T(8,128)}, s32[]{:T(128)}, s32[1,2,8]{2,1,0:T(2,128)S(1)}, bf16[32,12,96,96]{2,3,1,0:T(8,128)(2,1)}, /*ind...) while((s32[]{:T(128)}, f32[32,12,96,96]{2,3,1,0:T(8,128)}, ...), condition=%wide.region_2.4_spmd.clone.clone, body=%wide.region_0.3_spmd.clone.clone.sunk | while | flops 766734336 | bytes 18883840 | solution.py:92
  120.4 0.7 constant_dynamic-slice_fusion.4
  125.0 2.0 fusion.82
  127.1 0.8 convolution_bitcast_fusion.6
  127.9 0.2 copy.67
  128.1 0.2 reshape.214
  128.3 1.2 copy.68
  129.6 4.3 all-to-all-start
  133.8 0.2 fusion.81
  134.0 0.2 copy.66
  134.2 8.3 %all-to-all-done = f32[1,12,8,1152]{3,0,1,2:T(1,128)S(1)} async-done(((f32[1,12,8,1152]{3,0,1,2:T(1,128)}), f32[1,12,8,1152]{3,0,1,2:T(1,128)S(1)}, u32[]{:S(2)}, u32[]{:S(2)}) %all-to-all-start) | async-done | bytes 442400 | tf_op jit(solution)/shard_map/while/body/all_to_all | solution.py:68
  142.5 0.1 copy.70
  142.6 0.1 reshape.215
  142.7 0.8 fusion.83
  143.4 0.8 convolution_bitcast_fusion.7
  144.2 1.2 copy.71
  145.4 3.5 all-to-all-start.1
  148.9 0.8 and_reduce_fusion.2
  149.7 6.9 %all-to-all-done.1 = f32[1,96,1,1152]{3,2,0,1:T(1,128)S(1)} async-done(((f32[1,96,1,1152]{3,2,0,1:T(1,128)}), f32[1,96,1,1152]{3,2,0,1:T(1,128)S(1)}, u32[]{:S(2)}, u32[]{:S(2)}) %all-to-all-start.1) | async-done | bytes 442400 | tf_op jit(solution)/shard_map/while/body/all_to_all | solution.py:61
  156.6 0.2 reshape.216
  156.8 1.6 fusion.84
  158.5 3.4 fusion.85
  162.6 0.0 copy-start.1
  162.6 0.0 reduce-scatter.2.cloned.1.call-update
  162.6 463.6 %reduce-scatter.2.cloned.1.call-done = f32[1,12,96,96]{2,3,1,0:T(8,128)} async-done(((f32[32,12,96,96]{2,3,1,0:T(8,128)}), f32[1,12,96,96]{2,3,1,0:T(8,128)}) %reduce-scatter.2.cloned.1.call-update) | async-done | bytes 442384 | tf_op jit(solution)/shard_map/reduce_scatter | solution.py:93
  626.2 1.3 copy.53
  627.5 0.0 copy-done.1
  627.5 1.2 select_add_fusion
  (5 shorter events, 0.1 us)
Async XLA Ops:
  6.5 1.1 copy-start
  6.5 91.7 %all-gather.2.cloned.1.call-start = ((), (), s32[]{:S(2)}) async-start(), calls=%async_computation.3 | async-start | bytes 9732096 | tf_op jit(solution)/shard_map/all_gather | solution.py:51
  8.4 617.9 %reduce-scatter.2.cloned.1.call-start = ((), (), s32[]{:S(2)}) async-start(), calls=%async_computation.4 | async-start | bytes 19464192 | tf_op jit(solution)/shard_map/reduce_scatter | solution.py:93
  110.8 8.9 %copy-start.2 = (s32[1,2,8]{2,1,0:T(2,128)S(1)}, s32[1,2,8]{2,1,0:T(2,128)}, u32[]{:S(2)}) copy-start(s32[1,2,8]{2,1,0:T(2,128)} %param.14) | copy-start | bytes 196
  110.8 8.9 %copy-start.3 = (s32[4]{0:T(128)S(1)}, s32[4]{0:T(128)}, u32[]{:S(2)}) copy-start(s32[4]{0:T(128)} %constant.86.clone.3) | copy-start | bytes 52
  129.6 12.9 %all-to-all-start = ((f32[1,12,8,1152]{3,0,1,2:T(1,128)}), f32[1,12,8,1152]{3,0,1,2:T(1,128)S(1)}, u32[]{:S(2)}, u32[]{:S(2)}) async-start(f32[1,12,8,1152]{3,0,1,2:T(1,128)} %copy.68), calls=%async_computation | async-start | bytes 884736 | tf_op jit(solution)/shard_map/while/body/all_to_all | solution.py:68
  145.4 11.2 %all-to-all-start.1 = ((f32[1,96,1,1152]{3,2,0,1:T(1,128)}), f32[1,96,1,1152]{3,2,0,1:T(1,128)S(1)}, u32[]{:S(2)}, u32[]{:S(2)}) async-start(f32[1,96,1,1152]{3,2,0,1:T(1,128)} %copy.71), calls=%async_computation.1 | async-start | bytes 884736 | tf_op jit(solution)/shard_map/while/body/all_to_all | solution.py:61
  162.6 465.0 %copy-start.1 = (f32[2,12,96,96]{3,2,1,0:T(8,128)S(1)}, f32[2,12,96,96]{3,2,1,0:T(8,128)}, u32[]{:S(2)}) copy-start(f32[2,12,96,96]{3,2,1,0:T(8,128)} %param.12) | copy-start | bytes 2654212
Sparse Core Ops, SparseCore 0:
  9.9 88.2 all-gather.1
  162.7 463.4 reduce-scatter.1
where the time goes:
time: 638 us; the launch traced here: 636 us
  waiting for transfers between devices  568 us (89%)
  local copies, waits for them, and re-layouts  28.1 us (4%)
  between operations  14.2 us (2%)
  matrix products  9.39 us (1%)
  starting transfers between devices  7.77 us (1%)
    reduce_scatter x1, waiting for transfers between devices, on_device(): lax.psum_scatter(partial_value, 'band', scatter_dimension=0, tiled=True)  464 us
    all_gather x1, waiting for transfers between devices, on_device(): window = lax.all_gather(mine, 'band', axis=0, tiled=True)  89.6 us
    unnamed x9, local copies, waits for them, and re-layouts  13 us
  transfers between devices with their start and end apart: 4, of which 4 were waited for; matrix products, arithmetic and copies ran while one was open for 0% of the time, Pallas kernels for 0%

commit v1 on v0

v1 whole, which is shorter than its diff:
```python
import functools
import math

import jax
import jax.numpy as jnp
import numpy as np
from jax import lax
from jax.experimental import pallas as pl
from jax.experimental.pallas import tpu as pltpu
from jax.sharding import PartitionSpec as P

MESH = pl.DeviceIdType.MESH
LANES = 128
QUAD = 4


def hartley_table(length):
    steps_all = np.arange(length)
    angle = (steps_all[:, None] * steps_all[None, :] % length) * (2.0 * math.pi / length)
    return np.cos(angle) + np.sin(angle)


def split_table(length):
    table = hartley_table(length).astype(np.float32)
    high = table.astype(jnp.bfloat16)
    low = (table - high.astype(np.float32)).astype(jnp.bfloat16)
    return high, low


def lane_table(length):
    high, low = split_table(length)
    out = np.zeros((2 * LANES, 2 * LANES), jnp.bfloat16)
    out[:length, :length] = high
    out[:length, LANES : LANES + length] = low
    out[LANES : LANES + length, :length] = high
    return out


def row_table(length):
    high, low = split_table(length)
    out = np.zeros((2 * length, 2 * length), jnp.bfloat16)
    out[:length, :length] = high
    out[:length, length:] = high
    out[length:, :length] = low
    return out


def wavenumbers(length):
    steps_all = jnp.arange(length, dtype=jnp.int32)
    signed = jnp.where(steps_all <= length // 2, steps_all, steps_all - length)
    return signed.astype(jnp.float32) * (2.0 * math.pi / length)


def quarter_kernel(span, quarter):
    rows = span // QUAD
    wave = wavenumbers(span)
    second = lax.dynamic_slice_in_dim(wave, quarter * rows, rows)
    square = (wave * wave)[:, None, None] + (second * second)[None, :, None] + (wave * wave)[None, None, :]
    safe = jnp.where(square > 0, square, 1.0)
    kernel = jnp.where(square > 0, 4.0 * math.pi / span**3 / safe, 0.0)
    return jnp.pad(kernel, ((0, 0), (0, 0), (0, LANES - span))).reshape(span * rows, LANES)


def split(values):
    high = values.astype(jnp.bfloat16)
    return high, (values - high.astype(jnp.float32)).astype(jnp.bfloat16)


def along_lanes(values, table):
    both = jnp.dot(jnp.concatenate(split(values), axis=1), table, preferred_element_type=jnp.float32)
    return both[:, :LANES] + both[:, LANES:]


def along_rows(values, table):
    both = jnp.dot(table, jnp.concatenate(split(values), axis=0), preferred_element_type=jnp.float32)
    span = values.shape[0]
    return both[:span] + both[span:]


def task_kernel(
    quads, span, source_ref, target_ref, weight_ref, window_ref, kernel_ref, lane_ref, row_ref, out_ref,
    send_out, recv_out, send_back, recv_back, total, partner_part,
    out_send_sem, out_recv_sem, back_send_sem, back_recv_sem, part_sems,
):
    band = lax.axis_index("band")
    core = lax.rem(band, 2)
    pair = band - core
    members = 2 * lax.axis_size("grid")
    me = 2 * lax.axis_index("grid") + core
    own_rows = span // members
    rows = span // QUAD
    block = own_rows * rows

    def place(member):
        return {"band": pair + lax.rem(member, 2), "grid": member // 2}

    barrier = pltpu.get_barrier_semaphore()

    def greet(step, carry):
        pl.semaphore_signal(barrier, inc=1, device_id=place(lax.rem(me + step, members)), device_id_type=MESH)
        return carry

    lax.fori_loop(1, members, greet, 0)
    pl.semaphore_wait(barrier, members - 1)

    def at(ref, quad, member):
        return ref.at[quad, pl.ds(pl.multiple_of(member * block, 8), block)]

    def remote(quad, member, origin, src, dst, send_sem, recv_sem):
        return pltpu.make_async_remote_copy(
            src_ref=at(src, quad, member), dst_ref=at(dst, quad, origin),
            send_sem=send_sem.at[quad, member], recv_sem=recv_sem.at[quad, origin],
            device_id=place(member), device_id_type=MESH,
        )

    def local(quad, src, dst, recv_sem):
        return pltpu.make_async_copy(at(src, quad, me), at(dst, quad, me), recv_sem.at[quad, me])

    def start_all(quad, src, dst, send_sem, recv_sem):
        def step_one(step, carry):
            remote(quad, lax.rem(me + step, members), me, src, dst, send_sem, recv_sem).start()
            return carry

        lax.fori_loop(1, members, step_one, 0)
        local(quad, src, dst, recv_sem).start()

    def wait_recv(quad, src, dst, send_sem, recv_sem):
        def step_one(step, carry):
            other = lax.rem(me + step, members)
            remote(quad, other, other, src, dst, send_sem, recv_sem).wait_recv()
            return carry

        lax.fori_loop(1, members, step_one, 0)
        local(quad, src, dst, recv_sem).wait()

    def wait_send(quad, src, dst, send_sem, recv_sem):
        def step_one(step, carry):
            other = lax.rem(me + step, members)
            remote(quad, other, me, src, dst, send_sem, recv_sem).wait_send()
            return carry

        lax.fori_loop(1, members, step_one, 0)

    outward = (send_out, recv_out, out_send_sem, out_recv_sem)
    backward = (send_back, recv_back, back_send_sem, back_recv_sem)

    def inner(quad):
        def one(slot, carry):
            source, target = source_ref[quad * QUAD + slot], target_ref[quad * QUAD + slot]
            for two in range(own_rows // 2):
                part = pl.ds(2 * two * span, 2 * span)
                density = window_ref[source, part].astype(jnp.float32) * window_ref[target, part].astype(jnp.float32)
                mixed = along_lanes(density, lane_ref[...])
                mixed = along_rows(jnp.concatenate([mixed[:span], mixed[span:]], axis=1), row_ref[...])
                for quarter in range(QUAD):
                    for half in range(2):
                        start = (slot * QUAD + quarter) * block + (2 * two + half) * rows
                        send_out[quad, pl.ds(pl.multiple_of(start, 8), rows)] = mixed[
                            quarter * rows : (quarter + 1) * rows, half * LANES : (half + 1) * LANES
                        ]
            return carry

        lax.fori_loop(0, QUAD, one, 0)
        start_all(quad, *outward)

    def outer(quad):
        wait_recv(quad, *outward)

        def one(two, carry):
            picks = [pl.ds(2 * two + half, span, stride=rows) for half in range(2)]
            values = jnp.concatenate([recv_out[quad, pick] for pick in picks], axis=1)
            factor = jnp.concatenate([kernel_ref[pick] for pick in picks], axis=1)
            spectrum = along_rows(values, row_ref[...]) * factor
            restored = along_rows(spectrum, row_ref[...])
            for half in range(2):
                send_back[quad, picks[half]] = restored[:, half * LANES : (half + 1) * LANES]
            return carry

        lax.fori_loop(0, rows // 2, one, 0)
        start_all(quad, *backward)

    def finish(quad):
        wait_recv(quad, *backward)

        def one(slot, carry):
            source = source_ref[quad * QUAD + slot]
            weights = [weight_ref[side, quad * QUAD + slot] for side in range(2)]
            for two in range(own_rows // 2):
                halves = []
                for half in range(2):
                    starts = [(slot * QUAD + quarter) * block + (2 * two + half) * rows for quarter in range(QUAD)]
                    halves.append(
                        jnp.concatenate(
                            [recv_back[quad, pl.ds(pl.multiple_of(start, 8), rows)] for start in starts], axis=0
                        )
                    )
                mixed = along_rows(jnp.concatenate(halves, axis=1), row_ref[...])
                potential = along_lanes(
                    jnp.concatenate([mixed[:, :LANES], mixed[:, LANES:]], axis=0), lane_ref[...]
                )
                part = pl.ds(2 * two * span, 2 * span)
                action = potential * window_ref[source, part].astype(jnp.float32)
                for side in range(2):
                    total[side, part] += action * weights[side]
            return carry

        lax.fori_loop(0, QUAD, one, 0)

    total[...] = jnp.zeros_like(total)
    for quad in range(quads):
        inner(quad)
    for quad in range(quads):
        outer(quad)
        if quad > 0:
            finish(quad - 1)
    finish(quads - 1)

    swap = pltpu.make_async_remote_copy(
        src_ref=total.at[1 - core], dst_ref=partner_part, send_sem=part_sems.at[0], recv_sem=part_sems.at[1],
        device_id={"band": pair + 1 - core, "grid": lax.axis_index("grid")}, device_id_type=MESH,
    )
    swap.start()
    out_ref[core] = total[core]
    swap.wait_recv()
    out_ref[1 - core] = partner_part[...]
    swap.wait_send()
    for quad in range(quads):
        wait_send(quad, *outward)
        wait_send(quad, *backward)


def run_tasks(quads, span, members, sources, targets, weights, window, kernel, lane_constant, row_constant):
    own_rows = span // members
    whole = (quads, span * span // QUAD, LANES)
    smem, vmem = pl.BlockSpec(memory_space=pltpu.SMEM), pl.BlockSpec(memory_space=pltpu.VMEM)
    sems = pltpu.SemaphoreType.DMA((quads, members))
    return pl.pallas_call(
        functools.partial(task_kernel, quads, span),
        out_shape=jax.ShapeDtypeStruct((2, own_rows * span, LANES), jnp.float32),
        in_specs=[smem] * 3 + [vmem] * 4,
        out_specs=vmem,
        scratch_shapes=[pltpu.VMEM(whole, jnp.float32)] * 4
        + [pltpu.VMEM((2, own_rows * span, LANES), jnp.float32), pltpu.VMEM((own_rows * span, LANES), jnp.float32)]
        + [sems] * 4
        + [pltpu.SemaphoreType.DMA((2,))],
        compiler_params=pltpu.CompilerParams(
            collective_id=quads, has_side_effects=True, vmem_limit_bytes=56 * 1024 * 1024
        ),
        name="exchange_tasks",
    )(sources, targets, weights, window, kernel, lane_constant, row_constant)


def task_lists(task_pairs, task_count, groups, group):
    cap = task_pairs.shape[-1]
    mine = jnp.concatenate([task_pairs.reshape(2 * cap), task_count])
    every = lax.all_gather(mine, "band", axis=0, tiled=False)
    alive = jnp.arange(cap, dtype=jnp.int32)[None, :] < every[:, 2 * cap :]
    position = jnp.where(alive, every[:, cap : 2 * cap] * groups + every[:, :cap], -1).reshape(-1)
    entries = jnp.arange(groups * groups, dtype=jnp.int32)
    times = jnp.sum((position[:, None] == entries[None, :]).astype(jnp.int32), axis=0).reshape(-1, 2 * groups)
    live = times > 0
    most = jnp.max(jnp.sum(live.astype(jnp.int32), axis=1))
    own_times = lax.dynamic_index_in_dim(times, group, 0, keepdims=False)
    own_live = own_times > 0
    local = jnp.arange(2 * groups, dtype=jnp.int32)
    before = jnp.sum((own_live[None, :] & (local[None, :] < local[:, None])).astype(jnp.int32), axis=1)
    here = own_live[None, :] & (before[None, :] == local[:, None])
    entry = jnp.sum(jnp.where(here, local[None, :], 0), axis=1)
    often = jnp.sum(jnp.where(here, own_times[None, :], 0), axis=1).astype(jnp.float32)
    side = entry // groups
    weights = jnp.stack([jnp.where(side == 0, often, 0.0), jnp.where(side == 1, often, 0.0)])
    return entry % groups, 2 * group + side, weights, most


def on_device(orbitals, exchange_in, window_slot, task_pairs, task_count):
    band_dev, slab_rows, span, _ = orbitals.shape
    grid_parts = lax.axis_size("grid")
    groups = lax.axis_size("band")
    members = 2 * grid_parts
    own_rows = span // members
    band = lax.axis_index("band")
    core, group = band % 2, band // 2
    sources, targets, weights, most = task_lists(task_pairs, task_count, groups, group)

    mine = lax.dynamic_index_in_dim(orbitals, window_slot[0], 0, keepdims=False)
    mine = jnp.pad(mine.reshape(2, own_rows * span, span), ((0, 0), (0, 0), (0, LANES - span)))
    keep = lax.dynamic_index_in_dim(mine, core, 0)
    give = lax.dynamic_index_in_dim(mine, 1 - core, 0)
    got = lax.ppermute(give, "band", [(i, i ^ 1) for i in range(groups)])
    both = jnp.where(core == 0, jnp.concatenate([keep, got]), jnp.concatenate([got, keep]))
    window = lax.all_gather(
        both, "band", axis=0, tiled=True,
        axis_index_groups=[list(range(0, groups, 2)), list(range(1, groups, 2))],
    )

    member = 2 * lax.axis_index("grid") + core
    constants = (quarter_kernel(span, member % QUAD), jnp.asarray(lane_table(span)), jnp.asarray(row_table(span)))

    def few():
        return run_tasks(3, span, members, sources, targets, weights, window, *constants)

    def many():
        def step(carry):
            start, total = carry
            lists = [lax.dynamic_slice_in_dim(a, start, 16, a.ndim - 1) for a in (sources, targets, weights)]
            return start + 16, total + run_tasks(4, span, members, *lists, window, *constants)

        zero = jnp.zeros((2, own_rows * span, LANES), jnp.float32)
        return lax.while_loop(lambda carry: carry[0] < most, step, (jnp.int32(0), zero))[1]

    owned = lax.cond(most <= 12, few, many)
    owned = owned.reshape(slab_rows, span, LANES)[:, :, :span]
    slot_ids = jnp.arange(band_dev, dtype=jnp.int32)[:, None, None, None]
    return exchange_in + jnp.where(slot_ids == window_slot[0], owned, 0.0)


def solution(mesh):
    in_specs = (
        P("band", "grid", None, None),
        P("band", "grid", None, None),
        P("band"),
        P("band", None, None),
        P("band"),
    )
    out_specs = P("band", "grid", None, None)
    return jax.shard_map(
        on_device, mesh=mesh, in_specs=in_specs, out_specs=out_specs, check_vma=False
    )
```

time: 638 us -> 200 us (0.31)
  waiting for transfers between devices: 568 us -> 63.2 us
  Pallas kernels: 0 us -> 92.8 us
  local copies, waits for them, and re-layouts: 28.1 us -> 1.74 us
  blocking collectives: 0 us -> 16.1 us
  matrix products: 9.39 us -> 0 us
    reduce_scatter x1 -> x0, waiting for transfers between devices: 464 us -> none  [on_device(): lax.psum_scatter(partial_value, 'band', scatter_dimension=0, tiled=True)]
    pallas_call x0 -> x1, Pallas kernels: none -> 92.8 us  [run_tasks(): pl.pallas_call(functools.partial(task_kernel, quads, span), out_shape=jax...]
    all_gather x1, waiting for transfers between devices: 89.6 us -> 62.2 us  [on_device(): lax.all_gather(both, 'band', axis=0, tiled=True, axis_index_groups=[list(...]
    unnamed x0 -> x1, blocking collectives: none -> 16.1 us
    all_to_all x2 -> x0, waiting for transfers between devices: 15.2 us -> none  [the longest x1 8.25 us: potential_of(): lax.all_to_all(mixed, 'grid', split_axis=2, concat_axis=1, tiled=True)]
    unnamed x9 -> x12, local copies, waits for them, and re-layouts: 13 us -> 1.03 us
    broadcast_in_dim x2 -> x1, local copies, waits for them, and re-layouts: 10.2 us -> 0.01 us  [task_lists(): jnp.where(here, own_times[None, :], 0)]
    dot_general x6 -> x0, matrix products: 9.39 us -> none  [the longest x2 4.23 us: transform_inner(): jnp.einsum('bxyk,yj->bxjk', mixed, table_second, precision=lax.Precision....]
  transfers between devices with their start and end apart: 4 -> 2, of which waited for: 4 -> 2; matrix products, arithmetic and copies ran while one was open for 0% -> 2% of each run, Pallas kernels for 0% -> 0%
where the time goes in v1:
time: 200 us; the launch traced here: 199 us
  Pallas kernels  92.8 us (46%)
  waiting for transfers between devices  63.2 us (32%)
  between operations  16.2 us (8%)
  blocking collectives  16.1 us (8%)
  other arithmetic  5.28 us (3%)
  starting transfers between devices  3.33 us (2%)
    pallas_call x1, Pallas kernels, run_tasks(): pl.pallas_call(functools.partial(task_kernel, quads, span), out_shape=jax...  92.8 us
    all_gather x1, waiting for transfers between devices, on_device(): lax.all_gather(both, 'band', axis=0, tiled=True, axis_index_groups=[list(...  62.2 us
    unnamed x1, blocking collectives  16.1 us
  transfers between devices with their start and end apart: 2, of which 2 were waited for; matrix products, arithmetic and copies ran while one was open for 2% of the time, Pallas kernels for 0%

profile of v1, /device:TPU:1, one launch (start us, length us, event | category | flops | bytes accessed | tf_op | source)
XLA Modules:
  0.0 198.7 jit_solution(14638085562791277826)
XLA Ops:
  6.5 0.0 copy-start
  6.5 0.0 copy-start.4
  6.5 0.0 copy-start.3
  6.5 0.0 all-gather.3.cloned.1.call-start
  7.3 0.4 copy-done
  7.7 0.1 pad_dynamic-slice_fusion.1
  7.7 3.3 %collective-permute-start = (bf16[1,576,128]{2,1,0:T(8,128)(2,1)S(1)}, bf16[1,576,128]{2,1,0:T(8,128)(2,1)S(1)}, u32[]{:S(2)}, u32[]{:S(2)}) collective-permute-start(bf16[1,576,128]{2,1,0:T(8,128)(2,1)S(1)} %get-tuple-element.129), channel_id=1, source_target_pairs={{0,8},{8,0},{16,24},{24,16},{32,40},{40,32},{48,56},{56,48},{64,72... | collective-permute-start | bytes 442376 | tf_op jit(solution)/shard_map/ppermute | solution.py:289
  11.1 1.0 collective-permute-done
  12.1 0.7 maximum_select_fusion
  12.8 0.0 all-gather.3.cloned.1.call-update
  13.5 0.0 copy-done.3
  13.5 0.1 reshape.153
  13.6 0.0 copy-done.4
  13.6 0.6 dynamic-slice
  14.9 0.2 add_dynamic-update-slice_fusion
  15.1 16.1 %all-reduce.2 = s32[544]{0:T(1024)S(1)} all-reduce(s32[544]{0:T(1024)S(1)} %add_dynamic-update-slice_fusion), channel_id=2, replica_groups=mesh['band'=32,'grid'=8] {'band'}, use_global_device_ids=true, to_apply=%add.2 | all-reduce | flops 544 | bytes 4352
  31.2 0.1 reshape.158
  31.3 0.2 slice_reduce_fusion
  31.5 0.1 fusion.4
  31.5 0.1 eq.68
  31.6 0.2 convert_reduce_fusion
  31.8 0.1 reshape.154
  31.9 0.1 convert_reduce_fusion.2
  32.0 0.7 reduce_max.9
  33.3 0.1 dynamic-slice_multiply_fusion
  33.4 0.1 broadcast_add_fusion
  33.5 0.4 fusion
  33.9 0.0 copy-start.1
  33.9 0.0 copy-start.2
  33.9 0.1 pad.9
  34.0 0.1 convert_reduce_fusion.1
  34.2 0.1 select_reduce_fusion
  34.3 62.2 %all-gather.3.cloned.1.call-done = bf16[32,576,128]{2,1,0:T(8,128)(2,1)} async-done(((bf16[2,576,128]{2,1,0:T(8,128)(2,1)}), bf16[32,576,128]{2,1,0:T(8,128)(2,1)}) %all-gather.3.cloned.1.call-update) | async-done | bytes 4718608 | tf_op jit(solution)/shard_map/all_gather | solution.py:291
  96.6 0.0 copy-done.1
  96.6 0.0 copy-done.2
  96.6 92.8 %conditional.1 = (f32[2,576,128]{2,1,0:T(8,128)S(1)}) conditional(s32[]{:T(128)} %convert_element_type.50, (s32[]{:T(128)}, s32[64]{0:T(128)S(1)}, s32[64]{0:T(128)S(1)}, f32[2,64]{1,0:T(2,128)S(1)}, bf16[32,576,128]{2,1,0:T(8,128)(2,1)}, /*index=5*/f32[2304,128]{1,0:T(8,128)S(1)}, bf16[256,256]{1,0:T(8,128)(2,1)S(1)}, ...), branch_computations={%region_6.9_spmd, %region_9.10_spmd} | conditional | flops 147461 | bytes 2360111 | solution.py:311
  96.6 92.8 %exchange_tasks.2 = f32[2,576,128]{2,1,0:T(8,128)S(1)} custom-call(s32[64]{0:T(128)S(1)} %get-tuple-element.99.source_ref, s32[64]{0:T(128)S(1)} %get-tuple-element.100.target_ref, f32[2,64]{1,0:T(2,128)S(1)} %get-tuple-element.101.weight_ref, bf16[32,576,128]{2,1,0:T(8,128)(2,1)} %get-tuple-element.102.window_ref, ...), custom_call_target="tpu_custom_call" | custom-call | tf_op jit(solution)/shard_map/cond/branch_1_fun/exchange_tasks/pallas_call | solution.py:237
  189.4 2.5 %select_add_fusion = f32[2,12,96,96]{3,2,1,0:T(8,128)} fusion(f32[2,12,96,96]{3,2,1,0:T(8,128)} %param.12, f32[12,96,96]{2,1,0:T(8,128)S(1)} %bitcast.31, pred[2]{0:T(512)(128)(4,1)S(1)} %iota_compare_fusion.4), kind=kLoop, calls=%fused_computation.5 | loop fusion | flops 442368 | bytes 2211842 | tf_op jit(solution)/shard_map/add | solution.py:314
  (10 shorter events, 0.1 us)
Async XLA Ops:
  6.5 1.1 copy-start
  6.5 7.1 %copy-start.4 = (u32[256]{0:T(256)S(1)}, u32[256]{0:T(256)}, u32[]{:S(2)}) copy-start(u32[256]{0:T(256)} %constant.143) | copy-start | bytes 3076
  6.5 7.0 %copy-start.3 = (s32[1,2,8]{2,1,0:T(2,128)S(1)}, s32[1,2,8]{2,1,0:T(2,128)}, u32[]{:S(2)}) copy-start(s32[1,2,8]{2,1,0:T(2,128)} %param.14) | copy-start | bytes 196
  6.5 90.0 %all-gather.3.cloned.1.call-start = ((), (), s32[]{:S(2)}) async-start(), calls=%async_computation | async-start | bytes 5013504 | tf_op jit(solution)/shard_map/all_gather | solution.py:291
  7.7 4.3 %collective-permute-start = (bf16[1,576,128]{2,1,0:T(8,128)(2,1)S(1)}, bf16[1,576,128]{2,1,0:T(8,128)(2,1)S(1)}, u32[]{:S(2)}, u32[]{:S(2)}) collective-permute-start(bf16[1,576,128]{2,1,0:T(8,128)(2,1)S(1)} %get-tuple-element.129), channel_id=1, source_target_pairs={{0,8},{8,0},{16,24},{24,16},{32,40},{40,32},{48,56},{56,48},{64,72... | collective-permute-start | bytes 442376 | tf_op jit(solution)/shard_map/ppermute | solution.py:289
  33.9 62.7 %copy-start.1 = (bf16[256,256]{1,0:T(8,128)(2,1)S(1)}, bf16[256,256]{1,0:T(8,128)(2,1)}, u32[]{:S(2)}) copy-start(bf16[256,256]{1,0:T(8,128)(2,1)} %constant.130.clone) | copy-start | bytes 393220
  33.9 62.7 %copy-start.2 = (bf16[192,192]{1,0:T(8,128)(2,1)S(1)}, bf16[192,192]{1,0:T(8,128)(2,1)}, u32[]{:S(2)}) copy-start(bf16[192,192]{1,0:T(8,128)(2,1)} %constant.131.clone) | copy-start | bytes 221188
Sparse Core Ops, SparseCore 0:
  13.0 83.5 all-gather.2

commit v2 on v1

--- a/solution.py
+++ b/solution.py
@@ -36,12 +36,27 @@
     return out
 
 
-def row_table(length):
+def row_tables(length):
     high, low = split_table(length)
-    out = np.zeros((2 * length, 2 * length), jnp.bfloat16)
-    out[:length, :length] = high
-    out[:length, length:] = high
-    out[length:, :length] = low
+    order = np.concatenate([np.arange(0, length, 2), np.arange(1, length, 2)])
+    out = np.zeros((3, 2 * length, 2 * length), jnp.bfloat16)
+    plain = np.arange(length)
+    for which, pick in enumerate((np.ix_(plain, plain), np.ix_(plain, order), np.ix_(order, plain))):
+        out[which, :length, :length] = high[pick]
+        out[which, :length, length:] = high[pick]
+        out[which, length:, :length] = low[pick]
+    return out
+
+
+def emphasis(length):
+    steps_all = np.arange(length)
+    signed = np.where(steps_all <= length // 2, steps_all, steps_all - length).astype(np.float64)
+    return ((signed**2)[:, None] + (signed**2)[None, :] + 1.0) ** 0.75
+
+
+def undo_emphasis(length):
+    out = np.zeros((length, LANES), np.float32)
+    out[:, :length] = 1.0 / emphasis(length)
     return out
 
 
@@ -57,13 +72,72 @@
     second = lax.dynamic_slice_in_dim(wave, quarter * rows, rows)
     square = (wave * wave)[:, None, None] + (second * second)[None, :, None] + (wave * wave)[None, None, :]
     safe = jnp.where(square > 0, square, 1.0)
-    kernel = jnp.where(square > 0, 4.0 * math.pi / span**3 / safe, 0.0)
+    stress = lax.dynamic_slice_in_dim(jnp.asarray(emphasis(span), jnp.float32), quarter * rows, rows)
+    kernel = jnp.where(square > 0, 4.0 * math.pi / span**3 / safe, 0.0) * stress
     return jnp.pad(kernel, ((0, 0), (0, 0), (0, LANES - span))).reshape(span * rows, LANES)
 
 
 def split(values):
     high = values.astype(jnp.bfloat16)
     return high, (values - high.astype(jnp.float32)).astype(jnp.bfloat16)
+
+
+def unpack(values):
+    rows = values.shape[0] // 3
+    parts = [values[third * rows : (third + 1) * rows] for third in range(3)]
+    lane = lax.broadcasted_iota(jnp.int32, (rows, LANES), 1)
+    turned = [pltpu.roll(parts[third], 32 * (third + 1), 1) for third in range(3)]
+    last = jnp.where(lane < 32, turned[0], jnp.where(lane < 64, turned[1], turned[2]))
+    return jnp.concatenate([jnp.where(lane < 96, part, 0.0) for part in (*parts, last)], axis=0)
+
+
+LEVELS = 32766.0
+FINE = 2.0**24
+STEPS = 256.0
+LN2 = math.log(2.0)
+
+
+def grade(peak):
+    return jnp.ceil(jnp.log(jnp.maximum(peak, 1e-30)) * (STEPS / LN2) + 0.01)
+
+
+def size(graded):
+    return jnp.exp(graded * (LN2 / STEPS))
+
+
+def nearest(values):
+    return jnp.round(values).astype(jnp.int32)
+
+
+def encode(first, second, apart):
+    lane = lax.broadcasted_iota(jnp.int32, first.shape, 1)
+    if apart:
+        columns = (first[:, :1], second[:, :1])
+        first, second = jnp.where(lane > 0, first, 0.0), jnp.where(lane > 0, second, 0.0)
+    top = grade(jnp.max(jnp.maximum(jnp.abs(first), jnp.abs(second)), axis=(0, 1), keepdims=True))
+    factor = LEVELS / size(top)
+    word = nearest(first * factor) * 65536 + nearest(second * factor)
+    word = jnp.where(lane == 96, top.astype(jnp.int32), word)
+    if apart:
+        high = grade(jnp.max(jnp.maximum(jnp.abs(columns[0]), jnp.abs(columns[1])), axis=(0, 1), keepdims=True))
+        factor = FINE / size(high)
+        word = jnp.where(lane == 97, high.astype(jnp.int32), word)
+        word = jnp.where(lane == 98, nearest(columns[0] * factor), word)
+        word = jnp.where(lane == 99, nearest(columns[1] * factor), word)
+    return word
+
+
+def decode(word, apart):
+    second = lax.shift_right_arithmetic(lax.shift_left(word, 16), 16)
+    first = lax.shift_right_arithmetic(word - second, 16)
+    factor = size(word[:, 96:97].astype(jnp.float32)) * (1.0 / LEVELS)
+    first, second = first.astype(jnp.float32) * factor, second.astype(jnp.float32) * factor
+    if apart:
+        lane = lax.broadcasted_iota(jnp.int32, word.shape, 1)
+        factor = size(word[:, 97:98].astype(jnp.float32)) * (1.0 / FINE)
+        first = jnp.where(lane == 0, word[:, 98:99].astype(jnp.float32) * factor, first)
+        second = jnp.where(lane == 0, word[:, 99:100].astype(jnp.float32) * factor, second)
+    return first, second
 
 
 def along_lanes(values, table):
@@ -78,7 +152,7 @@
 
 
 def task_kernel(
-    quads, span, source_ref, target_ref, weight_ref, window_ref, kernel_ref, lane_ref, row_ref, out_ref,
+    quads, span, source_ref, target_ref, weight_ref, window_ref, kernel_ref, undo_ref, lane_ref, row_ref, out_ref,
     send_out, recv_out, send_back, recv_back, total, partner_part,
     out_send_sem, out_recv_sem, back_send_sem, back_recv_sem, part_sems,
 ):
@@ -89,7 +163,7 @@
     me = 2 * lax.axis_index("grid") + core
     own_rows = span // members
     rows = span // QUAD
-    block = own_rows * rows
+    block = own_rows // 2 * rows
 
     def place(member):
         return {"band": pair + lax.rem(member, 2), "grid": member // 2}
@@ -144,20 +218,22 @@
     outward = (send_out, recv_out, out_send_sem, out_recv_sem)
     backward = (send_back, recv_back, back_send_sem, back_recv_sem)
 
+    packed = window_ref.shape[1] // (own_rows // 2)
+
+    def window_part(position, two):
+        return window_ref[position, pl.ds(two * packed, packed)].astype(jnp.float32)
+
     def inner(quad):
         def one(slot, carry):
             source, target = source_ref[quad * QUAD + slot], target_ref[quad * QUAD + slot]
             for two in range(own_rows // 2):
-                part = pl.ds(2 * two * span, 2 * span)
-                density = window_ref[source, part].astype(jnp.float32) * window_ref[target, part].astype(jnp.float32)
-                mixed = along_lanes(density, lane_ref[...])
-                mixed = along_rows(jnp.concatenate([mixed[:span], mixed[span:]], axis=1), row_ref[...])
+                density = window_part(source, two) * window_part(target, two)
+                mixed = along_lanes(unpack(density), lane_ref[...])
+                mixed = along_rows(jnp.concatenate([mixed[:span], mixed[span:]], axis=1), row_ref[0])
+                word = encode(mixed[:, :LANES], mixed[:, LANES:], True)
                 for quarter in range(QUAD):
-                    for half in range(2):
-                        start = (slot * QUAD + quarter) * block + (2 * two + half) * rows
-                        send_out[quad, pl.ds(pl.multiple_of(start, 8), rows)] = mixed[
-                            quarter * rows : (quarter + 1) * rows, half * LANES : (half + 1) * LANES
-                        ]
+                    start = (slot * QUAD + quarter) * block + two * rows
+                    send_out[quad, pl.ds(pl.multiple_of(start, 8), rows)] = word[quarter * rows : (quarter + 1) * rows]
             return carry
 
         lax.fori_loop(0, QUAD, one, 0)
@@ -167,13 +243,14 @@
         wait_recv(quad, *outward)
 
         def one(two, carry):
-            picks = [pl.ds(2 * two + half, span, stride=rows) for half in range(2)]
-            values = jnp.concatenate([recv_out[quad, pick] for pick in picks], axis=1)
-            factor = jnp.concatenate([kernel_ref[pick] for pick in picks], axis=1)
-            spectrum = along_rows(values, row_ref[...]) * factor
-            restored = along_rows(spectrum, row_ref[...])
+            picks = [pl.ds(2 * two + half, span // 2, stride=rows) for half in range(2)]
+            values = [jnp.concatenate(decode(recv_out[quad, pick], True), axis=0) for pick in picks]
+            factors = [kernel_ref[pl.ds(2 * two + half, span, stride=rows)] for half in range(2)]
+            spectrum = along_rows(jnp.concatenate(values, axis=1), row_ref[1]) * jnp.concatenate(factors, axis=1)
+            restored = along_rows(spectrum, row_ref[2])
             for half in range(2):
-                send_back[quad, picks[half]] = restored[:, half * LANES : (half + 1) * LANES]
+                side = slice(half * LANES, (half + 1) * LANES)
+                send_back[quad, picks[half]] = encode(restored[: span // 2, side], restored[span // 2 :, side], False)
             return carry
 
         lax.fori_loop(0, rows // 2, one, 0)
@@ -186,20 +263,17 @@
             source = source_ref[quad * QUAD + slot]
             weights = [weight_ref[side, quad * QUAD + slot] for side in range(2)]
             for two in range(own_rows // 2):
-                halves = []
-                for half in range(2):
-                    starts = [(slot * QUAD + quarter) * block + (2 * two + half) * rows for quarter in range(QUAD)]
-                    halves.append(
-                        jnp.concatenate(
-                            [recv_back[quad, pl.ds(pl.multiple_of(start, 8), rows)] for start in starts], axis=0
-                        )
-                    )
-                mixed = along_rows(jnp.concatenate(halves, axis=1), row_ref[...])
+                starts = [(slot * QUAD + quarter) * block + two * rows for quarter in range(QUAD)]
+                word = jnp.concatenate(
+                    [recv_back[quad, pl.ds(pl.multiple_of(start, 8), rows)] for start in starts], axis=0
+                )
+                mixed = [half * undo_ref[...] for half in decode(word, False)]
+                mixed = along_rows(jnp.concatenate(mixed, axis=1), row_ref[0])
                 potential = along_lanes(
                     jnp.concatenate([mixed[:, :LANES], mixed[:, LANES:]], axis=0), lane_ref[...]
                 )
                 part = pl.ds(2 * two * span, 2 * span)
-                action = potential * window_ref[source, part].astype(jnp.float32)
+                action = potential * unpack(window_part(source, two))
                 for side in range(2):
                     total[side, part] += action * weights[side]
             return carry
@@ -229,17 +303,17 @@
         wait_send(quad, *backward)
 
 
-def run_tasks(quads, span, members, sources, targets, weights, window, kernel, lane_constant, row_constant):
+def run_tasks(quads, span, members, *operands):
     own_rows = span // members
-    whole = (quads, span * span // QUAD, LANES)
+    whole = (quads, span * span // QUAD // 2, LANES)
     smem, vmem = pl.BlockSpec(memory_space=pltpu.SMEM), pl.BlockSpec(memory_space=pltpu.VMEM)
     sems = pltpu.SemaphoreType.DMA((quads, members))
     return pl.pallas_call(
         functools.partial(task_kernel, quads, span),
         out_shape=jax.ShapeDtypeStruct((2, own_rows * span, LANES), jnp.float32),
-        in_specs=[smem] * 3 + [vmem] * 4,
+        in_specs=[smem] * 3 + [vmem] * 5,
         out_specs=vmem,
-        scratch_shapes=[pltpu.VMEM(whole, jnp.float32)] * 4
+        scratch_shapes=[pltpu.VMEM(whole, jnp.int32)] * 4
         + [pltpu.VMEM((2, own_rows * span, LANES), jnp.float32), pltpu.VMEM((own_rows * span, LANES), jnp.float32)]
         + [sems] * 4
         + [pltpu.SemaphoreType.DMA((2,))],
@@ -247,15 +321,171 @@
             collective_id=quads, has_side_effects=True, vmem_limit_bytes=56 * 1024 * 1024
         ),
         name="exchange_tasks",
-    )(sources, targets, weights, window, kernel, lane_constant, row_constant)
-
-
-def task_lists(task_pairs, task_count, groups, group):
-    cap = task_pairs.shape[-1]
-    mine = jnp.concatenate([task_pairs.reshape(2 * cap), task_count])
-    every = lax.all_gather(mine, "band", axis=0, tiled=False)
-    alive = jnp.arange(cap, dtype=jnp.int32)[None, :] < every[:, 2 * cap :]
-    position = jnp.where(alive, every[:, cap : 2 * cap] * groups + every[:, :cap], -1).reshape(-1)
+    )(*operands)
+
+
+def gather_kernel(
+    rings, span, orbital_ref, slot_ref, pairs_ref, count_ref, window_ref, lists_ref, give, own_list,
+    swap_sems, list_send, list_recv, near_send, near_recv, far_send, far_recv,
+):
+    ring_x, ring_z = rings
+    band = lax.axis_index("band")
+    groups = lax.axis_size("band")
+    core, chip = lax.rem(band, 2), band // 2
+    at_x, at_z = chip // ring_z, lax.rem(chip, ring_z)
+    packed = window_ref.shape[0] // groups
+
+    barrier = pltpu.get_barrier_semaphore()
+
+    def greet(step, carry):
+        pl.semaphore_signal(barrier, inc=1, device_id={"band": lax.rem(band + step, groups)}, device_id_type=MESH)
+        return carry
+
+    lax.fori_loop(1, groups, greet, 0)
+
+    part_rows = packed // 3
+    quarter = part_rows // 3
+    first = slot_ref[0] == 0
+    for two in range(3):
+        for side in range(2):
+            rows = pl.ds(side * (orbital_ref.shape[1] // 2) + two * 4 * quarter, 4 * quarter)
+            values = jnp.where(
+                first, orbital_ref[0, rows].astype(jnp.float32), orbital_ref[1, rows].astype(jnp.float32)
+            )
+            last = values[3 * quarter :]
+            for third in range(3):
+                full = jnp.concatenate(
+                    [values[third * quarter : (third + 1) * quarter], last[:, 32 * third : 32 * third + 32]], axis=1
+                ).astype(jnp.bfloat16)
+                row = two * part_rows + third * quarter
+
+                @pl.when(core == side)
+                def _():
+                    window_ref[pl.ds(pl.multiple_of(band * packed + row, 16), quarter)] = full
+
+                @pl.when(core != side)
+                def _():
+                    give[pl.ds(row, quarter)] = full
+
+    own_list[...] = jnp.zeros_like(own_list)
+    own_list[0:2, 0 : pairs_ref.shape[1]] = pairs_ref[...]
+    own_list[2:3] = jnp.full((1, LANES), count_ref[0], jnp.int32)
+
+    pl.semaphore_wait(barrier, groups - 1)
+
+    def blocks(first_band, count):
+        return window_ref.at[pl.ds(pl.multiple_of(first_band * packed, 16), count * packed)]
+
+    def send(src, dst, send_sem, recv_sem, target):
+        return pltpu.make_async_remote_copy(
+            src_ref=src, dst_ref=dst, send_sem=send_sem, recv_sem=recv_sem,
+            device_id={"band": target}, device_id_type=MESH,
+        )
+
+    def swap(owner):
+        return send(give, blocks(owner, 1), swap_sems.at[0], swap_sems.at[1], band + 1 - 2 * core)
+
+    swap(band).start()
+
+    def send_list(step, owner):
+        other = lax.rem(band + step, groups)
+        return send(own_list, lists_ref.at[owner], list_send.at[step], list_recv.at[step], other)
+
+    def start_list(step, carry):
+        send_list(step, band).start()
+        return carry
+
+    def place(x, z):
+        return lax.rem(x + ring_x, ring_x) * ring_z + lax.rem(z + ring_z, ring_z)
+
+    level = (0, -1, 1, 2)
+
+    def along(ring, step):
+        if ring == 0:
+            return place(at_x, at_z + step)
+        return place(at_x + step, at_z + level[ring - 1])
+
+    def neighbour(ring, step):
+        target = place(at_x, at_z + step) if ring == 0 else place(at_x + step, at_z)
+        return 2 * target + core
+
+    def near(ring, way):
+        block = blocks(2 * along(ring, 0), 2)
+        return send(block, block, near_send.at[ring, way], near_recv.at[ring, way], neighbour(ring, 1 - 2 * way))
+
+    def far(ring, way):
+        block = blocks(2 * along(ring, -1 + 2 * way) + way, 1)
+        return send(block, block, far_send.at[ring, way], far_recv.at[ring, way], neighbour(ring, 1 - 2 * way))
+
+    def begin(ring):
+        for way in range(2):
+            near(ring, way).start()
+
+    def onward(ring):
+        for way in range(2):
+            near(ring, way).wait_recv()
+            far(ring, way).start()
+
+    swap(band).wait_recv()
+    begin(0)
+    begin(1)
+    lax.fori_loop(1, groups, start_list, 0)
+    for way in range(2):
+        near(0, way).wait_recv()
+        far(0, way).start()
+        begin(2 + way)
+    onward(1)
+    for way in range(2):
+        far(0, way).wait_recv()
+    begin(4)
+    onward(2)
+    onward(3)
+    onward(4)
+    for ring in range(1, 5):
+        for way in range(2):
+            far(ring, way).wait_recv()
+
+    def end_list(step, carry):
+        send_list(step, band).wait_recv()
+        send_list(step, band).wait_send()
+        return carry
+
+    lax.fori_loop(1, groups, end_list, 0)
+    lists_ref[band] = own_list[...]
+    swap(band).wait_send()
+    for ring in range(5):
+        for way in range(2):
+            near(ring, way).wait_send()
+            far(ring, way).wait_send()
+
+
+def gather_window(rings, span, orbitals, window_slot, task_pairs, task_count):
+    groups = lax.axis_size("band")
+    slab_rows = orbitals.shape[1]
+    packed = slab_rows // 2 * span * span // LANES
+    smem, vmem = pl.BlockSpec(memory_space=pltpu.SMEM), pl.BlockSpec(memory_space=pltpu.VMEM)
+    dma = pltpu.SemaphoreType.DMA
+    return pl.pallas_call(
+        functools.partial(gather_kernel, rings, span),
+        out_shape=(
+            jax.ShapeDtypeStruct((groups * packed, LANES), jnp.bfloat16),
+            jax.ShapeDtypeStruct((groups, 8, LANES), jnp.int32),
+        ),
+        in_specs=[vmem, smem, vmem, smem],
+        out_specs=(vmem, vmem),
+        scratch_shapes=[pltpu.VMEM((packed, LANES), jnp.bfloat16), pltpu.VMEM((8, LANES), jnp.int32)]
+        + [dma((2,)), dma((groups,)), dma((groups,))]
+        + [dma((5, 2))] * 4,
+        compiler_params=pltpu.CompilerParams(
+            collective_id=9, has_side_effects=True, vmem_limit_bytes=56 * 1024 * 1024
+        ),
+        name="gather_window",
+    )(orbitals.reshape(2, slab_rows * span, span), window_slot, task_pairs[0], task_count)
+
+
+def task_lists(lists, cap, groups, group):
+    alive = jnp.arange(cap, dtype=jnp.int32)[None, :] < lists[:, 2, :1]
+    position = jnp.where(alive, lists[:, 1, :cap] * groups + lists[:, 0, :cap], -1).reshape(-1)
     entries = jnp.arange(groups * groups, dtype=jnp.int32)
     times = jnp.sum((position[:, None] == entries[None, :]).astype(jnp.int32), axis=0).reshape(-1, 2 * groups)
     live = times > 0
@@ -280,21 +510,15 @@
     own_rows = span // members
     band = lax.axis_index("band")
     core, group = band % 2, band // 2
-    sources, targets, weights, most = task_lists(task_pairs, task_count, groups, group)
-
-    mine = lax.dynamic_index_in_dim(orbitals, window_slot[0], 0, keepdims=False)
-    mine = jnp.pad(mine.reshape(2, own_rows * span, span), ((0, 0), (0, 0), (0, LANES - span)))
-    keep = lax.dynamic_index_in_dim(mine, core, 0)
-    give = lax.dynamic_index_in_dim(mine, 1 - core, 0)
-    got = lax.ppermute(give, "band", [(i, i ^ 1) for i in range(groups)])
-    both = jnp.where(core == 0, jnp.concatenate([keep, got]), jnp.concatenate([got, keep]))
-    window = lax.all_gather(
-        both, "band", axis=0, tiled=True,
-        axis_index_groups=[list(range(0, groups, 2)), list(range(1, groups, 2))],
+    window, lists = gather_window((4, 4), span, orbitals, window_slot, task_pairs, task_count)
+    sources, targets, weights, most = task_lists(lists, task_pairs.shape[-1], groups, group)
+
+    window = window.reshape(groups, -1, LANES)
+    member = 2 * lax.axis_index("grid") + core
+    constants = (
+        quarter_kernel(span, member % QUAD), jnp.asarray(undo_emphasis(span)), jnp.asarray(lane_table(span)),
+        jnp.asarray(row_tables(span)),
     )
-
-    member = 2 * lax.axis_index("grid") + core
-    constants = (quarter_kernel(span, member % QUAD), jnp.asarray(lane_table(span)), jnp.asarray(row_table(span)))
 
     def few():
         return run_tasks(3, span, members, sources, targets, weights, window, *constants)

time: 200 us -> 157 us (0.79)
  waiting for transfers between devices: 63.2 us -> 0 us
  Pallas kernels: 92.8 us -> 135 us
  blocking collectives: 16.1 us -> 0 us
  between operations: 16.2 us -> 2 us
  local copies, waits for them, and re-layouts: 1.74 us -> 8.27 us
  other arithmetic: 5.28 us -> 9.78 us
  starting transfers between devices: 3.33 us -> 0 us
    all_gather x1 -> x0, waiting for transfers between devices: 62.2 us -> none  [on_device(): lax.all_gather(both, 'band', axis=0, tiled=True, axis_index_groups=[list(...]
    pallas_call x0 -> x1, Pallas kernels: none -> 48 us  [gather_window(): pl.pallas_call(functools.partial(gather_kernel, rings, span), out_shape=(...]
    unnamed x1 -> x0, blocking collectives: 16.1 us -> none
    pallas_call x1, Pallas kernels: 92.8 us -> 87.1 us  [run_tasks(): pl.pallas_call(functools.partial(task_kernel, quads, span), out_shape=jax...]
    ppermute x1 -> x0, starting transfers between devices: 3.33 us -> none  [on_device(): got = lax.ppermute(give, 'band', [(i, i ^ 1) for i in range(groups)])]
    dynamic_slice x2 -> x4, local copies, waits for them, and re-layouts: 0.09 us -> 2.59 us  [the longest x3 1.88 us: step(): lax.dynamic_slice_in_dim(a, start, 16, a.ndim - 1)]
    add x0 -> x2, other arithmetic: none -> 2.22 us  [the longest x1 1.18 us: step(): total + run_tasks(4, span, members, *lists, window, *constants)]
  transfers between devices with their start and end apart: 2 -> 0, of which waited for: 2 -> 0; matrix products, arithmetic and copies ran while one was open for 2% -> 0% of each run, Pallas kernels for 0% -> 0%
where the time goes in v2:
time: 157 us
  Pallas kernels  135 us (86%)
  other arithmetic  9.78 us (6%)
  local copies, waits for them, and re-layouts  8.27 us (5%)
  between operations  2 us (1%)
    pallas_call x1, Pallas kernels, run_tasks(): pl.pallas_call(functools.partial(task_kernel, quads, span), out_shape=jax...  87.1 us
    pallas_call x1, Pallas kernels, gather_window(): pl.pallas_call(functools.partial(gather_kernel, rings, span), out_shape=(...  48 us

profile of v2, /device:TPU:1, one launch (start us, length us, event | category | flops | bytes accessed | tf_op | source)
XLA Modules:
  0.0 156.7 jit_solution(11879444718093385332)
XLA Ops:
  1.3 0.5 iota_compare_fusion.4
  1.9 0.1 dynamic-slice_multiply_fusion
  1.9 0.7 constant_dynamic-slice_fusion.1
  2.6 0.1 broadcast_add_fusion
  2.7 0.4 fusion.1
  3.1 1.1 pad.4
  4.2 48.0 %gather_window.1 = (bf16[13824,128]{1,0:T(8,128)(2,1)S(1)}, s32[32,8,128]{2,1,0:T(8,128)}) custom-call(bf16[2,1152,96]{2,1,0:T(8,128)(2,1)} %bitcast.32, s32[1]{0:T(128)} %copy.18.slot_ref, s32[2,8]{1,0:T(2,128)} %bitcast.33, s32[1]{0:T(128)S(6)} %copy.19.count_ref), custom_call_target="tpu_custom_call" | custom-call | tf_op jit(solution)/shard_map/gather_window/pallas_call | solution.py:468
  52.2 2.1 %slice_reduce_fusion = s32[32]{0:T(128)} fusion(s32[32,8,128]{2,1,0:T(8,128)} %get-tuple-element.119), kind=kLoop, calls=%fused_computation.18 | loop fusion | bytes 256 | tf_op jit(solution)/shard_map/slice | solution.py:487
  54.3 1.0 add_reduce_fusion
  55.3 0.7 add.110
  56.0 0.7 iota_compare_fusion.3
  56.7 0.1 lt.75
  56.8 0.7 broadcast_select_fusion
  57.5 0.2 convert_reduce_fusion
  57.7 0.1 reshape.182
  57.8 0.7 convert_reduce_fusion.2
  58.5 1.3 reduce_max.9
  60.4 0.1 convert_reduce_fusion.1
  60.5 0.1 select_reduce_fusion
  60.7 0.0 copy-start.2
  60.7 93.3 %conditional.1 = (f32[2,576,128]{2,1,0:T(8,128)}) conditional(s32[]{:T(128)} %convert_element_type.48, (s32[]{:T(128)}, s32[64]{0:T(128)S(1)}, s32[64]{0:T(128)S(1)}, f32[2,64]{1,0:T(2,128)S(1)}, bf16[32,432,128]{2,1,0:T(8,128)(2,1)S(1)}, /*index=5*/f32[2304,128]{1,0:T(8,128)}, f32[96,128]{1,0:T(8,128)}, bf16[256,256]{1,0:T(8,128)(2,1)}, ...), branch_computations={%region_6.9_spmd, %region_9.10_spmd} | conditional | flops 147461 | bytes 7078775 | solution.py:535
  60.7 0.8 broadcast.187
  61.6 92.3 %while.9 = (s32[]{:T(128)}, f32[2,576,128]{2,1,0:T(8,128)}, s32[]{:T(128)}, s32[64]{0:T(128)S(1)}, s32[64]{0:T(128)S(1)}, /*index=5*/f32[2,64]{1,0:T(2,128)S(1)}...) while((s32[]{:T(128)}, f32[2,576,128]{2,1,0:T(8,128)}, ...), condition=%wide.region_8.8_spmd, body=%wide.region_7.7_spmd.sunk | while | flops 147461 | bytes 6488819 | solution.py:533
  62.2 0.7 dynamic_slice.35.target_ref
  62.9 0.6 dynamic_slice.34.source_ref
  63.4 0.6 constant_dynamic-slice_fusion.4.weight_ref
  64.1 0.0 copy-start
  64.1 87.1 %exchange_tasks.3 = f32[2,576,128]{2,1,0:T(8,128)} custom-call(s32[16]{0:T(128)} %dynamic_slice.34.source_ref, s32[16]{0:T(128)} %dynamic_slice.35.target_ref, f32[2,16]{1,0:T(2,128)} %constant_dynamic-slice_fusion.4.weight_ref, bf16[32,432,128]{2,1,0:T(8,128)(2,1)S(1)} %get-tuple-element.251.window_ref, f32[2304,128]{1,0:T(8,128)} %get-tuple-element.252.kernel_ref, ...), custom_call_target="tpu_custom_call" | custom-call | tf_op jit(solution)/shard_map/cond/branch_0_fun/while/body/exchange_tasks/pallas_call | solution.py:311
  151.2 0.0 copy-done
  151.2 1.2 add.157
  152.4 0.0 copy-start.1
  152.4 0.8 copy-done.1
  154.0 0.0 copy-done.2
  154.1 2.6 %select_add_fusion = f32[2,12,96,96]{3,2,1,0:T(8,128)} fusion(f32[2,12,96,96]{3,2,1,0:T(8,128)} %param.14, f32[12,96,96]{2,1,0:T(8,128)} %bitcast.31, pred[2]{0:T(512)(128)(4,1)S(1)} %copy-done.2), kind=kLoop, calls=%fused_computation.6 | loop fusion | flops 442368 | bytes 2211842 | tf_op jit(solution)/shard_map/add | solution.py:538
  (7 shorter events, 0.1 us)
Async XLA Ops:
  60.7 93.3 %copy-start.2 = (pred[2]{0:T(512)(128)(4,1)S(1)}, pred[2]{0:T(512)(128)(4,1)}, u32[]{:S(2)}) copy-start(pred[2]{0:T(512)(128)(4,1)} %iota_compare_fusion.4) | copy-start | bytes 10
  64.1 87.2 %copy-start = (f32[2,576,128]{2,1,0:T(8,128)S(1)}, f32[2,576,128]{2,1,0:T(8,128)}, u32[]{:S(2)}) copy-start(f32[2,576,128]{2,1,0:T(8,128)} %get-tuple-element.232) | copy-start | bytes 1769476 | tf_op jit(solution)/shard_map/cond/branch_0_fun/while
  152.4 0.8 copy-start.1

commit v3 on v2

--- a/solution.py
+++ b/solution.py
@@ -12,6 +12,7 @@
 MESH = pl.DeviceIdType.MESH
 LANES = 128
 QUAD = 4
+UNROLL = 3
 
 
 def hartley_table(length):
@@ -60,21 +61,14 @@
     return out
 
 
-def wavenumbers(length):
-    steps_all = jnp.arange(length, dtype=jnp.int32)
-    signed = jnp.where(steps_all <= length // 2, steps_all, steps_all - length)
-    return signed.astype(jnp.float32) * (2.0 * math.pi / length)
-
-
-def quarter_kernel(span, quarter):
-    rows = span // QUAD
-    wave = wavenumbers(span)
-    second = lax.dynamic_slice_in_dim(wave, quarter * rows, rows)
-    square = (wave * wave)[:, None, None] + (second * second)[None, :, None] + (wave * wave)[None, None, :]
-    safe = jnp.where(square > 0, square, 1.0)
-    stress = lax.dynamic_slice_in_dim(jnp.asarray(emphasis(span), jnp.float32), quarter * rows, rows)
-    kernel = jnp.where(square > 0, 4.0 * math.pi / span**3 / safe, 0.0) * stress
-    return jnp.pad(kernel, ((0, 0), (0, 0), (0, LANES - span))).reshape(span * rows, LANES)
+def quarter_kernels(span):
+    steps_all = np.arange(span)
+    wave = np.where(steps_all <= span // 2, steps_all, steps_all - span) * (2.0 * math.pi / span)
+    square = (wave**2)[:, None, None] + (wave**2)[None, :, None] + (wave**2)[None, None, :]
+    safe = np.where(square > 0, square, 1.0)
+    kernel = np.where(square > 0, 4.0 * math.pi / span**3 / safe, 0.0) * emphasis(span)
+    kernel = np.pad(kernel, ((0, 0), (0, 0), (0, LANES - span))).reshape(span, QUAD, span // QUAD, LANES)
+    return kernel.transpose(1, 0, 2, 3).reshape(QUAD, -1, LANES).astype(np.float32)
 
 
 def split(values):
@@ -109,35 +103,51 @@
     return jnp.round(values).astype(jnp.int32)
 
 
-def encode(first, second, apart):
+def encode(first, second):
     lane = lax.broadcasted_iota(jnp.int32, first.shape, 1)
-    if apart:
-        columns = (first[:, :1], second[:, :1])
-        first, second = jnp.where(lane > 0, first, 0.0), jnp.where(lane > 0, second, 0.0)
     top = grade(jnp.max(jnp.maximum(jnp.abs(first), jnp.abs(second)), axis=(0, 1), keepdims=True))
     factor = LEVELS / size(top)
     word = nearest(first * factor) * 65536 + nearest(second * factor)
-    word = jnp.where(lane == 96, top.astype(jnp.int32), word)
-    if apart:
-        high = grade(jnp.max(jnp.maximum(jnp.abs(columns[0]), jnp.abs(columns[1])), axis=(0, 1), keepdims=True))
-        factor = FINE / size(high)
-        word = jnp.where(lane == 97, high.astype(jnp.int32), word)
-        word = jnp.where(lane == 98, nearest(columns[0] * factor), word)
-        word = jnp.where(lane == 99, nearest(columns[1] * factor), word)
-    return word
-
-
-def decode(word, apart):
+    return jnp.where(lane == 96, top.astype(jnp.int32), word)
+
+
+def encode_apart(first, second):
+    lane = lax.broadcasted_iota(jnp.int32, (1, LANES), 1)
+    peaks = jnp.max(jnp.maximum(jnp.abs(first), jnp.abs(second)), axis=0, keepdims=True)
+    top = grade(jnp.max(jnp.where(lane > 0, peaks, 0.0), axis=1, keepdims=True))
+    high = grade(jnp.max(jnp.where(lane > 0, 0.0, peaks), axis=1, keepdims=True))
+    factor = jnp.where(lane > 0, LEVELS / size(top), FINE / size(high))
+    first, second = nearest(first * factor), nearest(second * factor)
+    lane = lax.broadcasted_iota(jnp.int32, first.shape, 1)
+    word = jnp.where(lane > 0, first * 65536 + second, first)
+    word = jnp.where(lane == 96, pltpu.roll(second, 96, 1), word)
+    return jnp.where(lane == 97, top.astype(jnp.int32), jnp.where(lane == 98, high.astype(jnp.int32), word))
+
+
+def halves(word):
     second = lax.shift_right_arithmetic(lax.shift_left(word, 16), 16)
-    first = lax.shift_right_arithmetic(word - second, 16)
-    factor = size(word[:, 96:97].astype(jnp.float32)) * (1.0 / LEVELS)
-    first, second = first.astype(jnp.float32) * factor, second.astype(jnp.float32) * factor
-    if apart:
-        lane = lax.broadcasted_iota(jnp.int32, word.shape, 1)
-        factor = size(word[:, 97:98].astype(jnp.float32)) * (1.0 / FINE)
-        first = jnp.where(lane == 0, word[:, 98:99].astype(jnp.float32) * factor, first)
-        second = jnp.where(lane == 0, word[:, 99:100].astype(jnp.float32) * factor, second)
-    return first, second
+    return lax.shift_right_arithmetic(word - second, 16), second
+
+
+def scale_of(word):
+    return size(word[:, 96:97].astype(jnp.float32)) * (1.0 / LEVELS)
+
+
+def decode(word, scale):
+    return [half.astype(jnp.float32) * scale for half in halves(word)]
+
+
+def scale_apart(word):
+    lane = lax.broadcasted_iota(jnp.int32, word.shape, 1)
+    rest = size(word[:, 97:98].astype(jnp.float32)) * (1.0 / LEVELS)
+    return jnp.where(lane > 0, rest, size(word[:, 98:99].astype(jnp.float32)) * (1.0 / FINE))
+
+
+def decode_apart(word, scale):
+    lane = lax.broadcasted_iota(jnp.int32, word.shape, 1)
+    first, second = halves(word)
+    first, second = jnp.where(lane > 0, first, word), jnp.where(lane > 0, second, pltpu.roll(word, 32, 1))
+    return [first.astype(jnp.float32) * scale, second.astype(jnp.float32) * scale]
 
 
 def along_lanes(values, table):
@@ -152,9 +162,9 @@
 
 
 def task_kernel(
-    quads, span, source_ref, target_ref, weight_ref, window_ref, kernel_ref, undo_ref, lane_ref, row_ref, out_ref,
-    send_out, recv_out, send_back, recv_back, total, partner_part,
-    out_send_sem, out_recv_sem, back_send_sem, back_recv_sem, part_sems,
+    quads, span, start_ref, list_ref, window_ref, kernels_ref, undo_ref, lane_ref, row_ref, out_ref,
+    kernel_ref, send_out, recv_out, send_back, recv_back, total, partner_part,
+    out_send_sem, out_recv_sem, back_send_sem, back_recv_sem, part_sems, kernel_sem,
 ):
     band = lax.axis_index("band")
     core = lax.rem(band, 2)
@@ -168,6 +178,8 @@
     def place(member):
         return {"band": pair + lax.rem(member, 2), "grid": member // 2}
 
+    kernel_copy = pltpu.make_async_copy(kernels_ref.at[lax.rem(me, QUAD)], kernel_ref, kernel_sem.at[0])
+    kernel_copy.start()
     barrier = pltpu.get_barrier_semaphore()
 
     def greet(step, carry):
@@ -175,7 +187,6 @@
         return carry
 
     lax.fori_loop(1, members, greet, 0)
-    pl.semaphore_wait(barrier, members - 1)
 
     def at(ref, quad, member):
         return ref.at[quad, pl.ds(pl.multiple_of(member * block, 8), block)]
@@ -223,51 +234,72 @@
     def window_part(position, two):
         return window_ref[position, pl.ds(two * packed, packed)].astype(jnp.float32)
 
+    def task(quad, slot):
+        index = start_ref[0] + quad * QUAD + slot
+        entry = list_ref[0, index]
+        groups = lax.axis_size("band")
+        return lax.rem(entry, groups), entry // groups, list_ref[1, index].astype(jnp.float32)
+
     def inner(quad):
         def one(slot, carry):
-            source, target = source_ref[quad * QUAD + slot], target_ref[quad * QUAD + slot]
+            source, side, _ = task(quad, slot)
+            target = pair + side
             for two in range(own_rows // 2):
                 density = window_part(source, two) * window_part(target, two)
                 mixed = along_lanes(unpack(density), lane_ref[...])
                 mixed = along_rows(jnp.concatenate([mixed[:span], mixed[span:]], axis=1), row_ref[0])
-                word = encode(mixed[:, :LANES], mixed[:, LANES:], True)
+                word = encode_apart(mixed[:, :LANES], mixed[:, LANES:])
                 for quarter in range(QUAD):
                     start = (slot * QUAD + quarter) * block + two * rows
                     send_out[quad, pl.ds(pl.multiple_of(start, 8), rows)] = word[quarter * rows : (quarter + 1) * rows]
             return carry
 
         lax.fori_loop(0, QUAD, one, 0)
-        start_all(quad, *outward)
 
     def outer(quad):
         wait_recv(quad, *outward)
-
-        def one(two, carry):
-            picks = [pl.ds(2 * two + half, span // 2, stride=rows) for half in range(2)]
-            values = [jnp.concatenate(decode(recv_out[quad, pick], True), axis=0) for pick in picks]
-            factors = [kernel_ref[pl.ds(2 * two + half, span, stride=rows)] for half in range(2)]
-            spectrum = along_rows(jnp.concatenate(values, axis=1), row_ref[1]) * jnp.concatenate(factors, axis=1)
-            restored = along_rows(spectrum, row_ref[2])
-            for half in range(2):
-                side = slice(half * LANES, (half + 1) * LANES)
-                send_back[quad, picks[half]] = encode(restored[: span // 2, side], restored[span // 2 :, side], False)
+        scale = scale_apart(recv_out[quad, pl.ds(0, span // 2, stride=rows)])
+
+        def some(step, carry):
+            pairs = [step * UNROLL + i for i in range(UNROLL)]
+            picks = [[pl.ds(2 * two + half, span // 2, stride=rows) for half in range(2)] for two in pairs]
+            words = [[recv_out[quad, pick] for pick in both] for both in picks]
+            values = [
+                jnp.concatenate([jnp.concatenate(decode_apart(word, scale), axis=0) for word in both], axis=1)
+                for both in words
+            ]
+            mixed = [along_rows(value, row_ref[1]) for value in values]
+            factors = [
+                jnp.concatenate([kernel_ref[pl.ds(2 * two + half, span, stride=rows)] for half in range(2)], axis=1)
+                for two in pairs
+            ]
+            restored = [along_rows(value * factor, row_ref[2]) for value, factor in zip(mixed, factors)]
+            sides = [slice(half * LANES, (half + 1) * LANES) for half in range(2)]
+            words = [[encode(value[: span // 2, side], value[span // 2 :, side]) for side in sides] for value in restored]
+            for both, pair_words in zip(picks, words):
+                for pick, word in zip(both, pair_words):
+                    send_back[quad, pick] = word
             return carry
 
-        lax.fori_loop(0, rows // 2, one, 0)
+        lax.fori_loop(0, rows // 2 // UNROLL, some, 0)
         start_all(quad, *backward)
 
     def finish(quad):
         wait_recv(quad, *backward)
 
         def one(slot, carry):
-            source = source_ref[quad * QUAD + slot]
-            weights = [weight_ref[side, quad * QUAD + slot] for side in range(2)]
-            for two in range(own_rows // 2):
+            source, wanted, often = task(quad, slot)
+            weights = [jnp.where(wanted == side, often, 0.0) for side in range(2)]
+
+            def arrived(two):
                 starts = [(slot * QUAD + quarter) * block + two * rows for quarter in range(QUAD)]
-                word = jnp.concatenate(
+                return jnp.concatenate(
                     [recv_back[quad, pl.ds(pl.multiple_of(start, 8), rows)] for start in starts], axis=0
                 )
-                mixed = [half * undo_ref[...] for half in decode(word, False)]
+
+            scale = scale_of(arrived(0)) * undo_ref[...]
+            for two in range(own_rows // 2):
+                mixed = decode(arrived(two), scale)
                 mixed = along_rows(jnp.concatenate(mixed, axis=1), row_ref[0])
                 potential = along_lanes(
                     jnp.concatenate([mixed[:, :LANES], mixed[:, LANES:]], axis=0), lane_ref[...]
@@ -283,6 +315,10 @@
     total[...] = jnp.zeros_like(total)
     for quad in range(quads):
         inner(quad)
+        if quad == 0:
+            pl.semaphore_wait(barrier, members - 1)
+        start_all(quad, *outward)
+    kernel_copy.wait()
     for quad in range(quads):
         outer(quad)
         if quad > 0:
@@ -311,12 +347,13 @@
     return pl.pallas_call(
         functools.partial(task_kernel, quads, span),
         out_shape=jax.ShapeDtypeStruct((2, own_rows * span, LANES), jnp.float32),
-        in_specs=[smem] * 3 + [vmem] * 5,
+        in_specs=[smem] * 2 + [vmem] + [pl.BlockSpec(memory_space=pl.ANY)] + [vmem] * 3,
         out_specs=vmem,
-        scratch_shapes=[pltpu.VMEM(whole, jnp.int32)] * 4
+        scratch_shapes=[pltpu.VMEM((span * span // QUAD, LANES), jnp.float32)]
+        + [pltpu.VMEM(whole, jnp.int32)] * 4
         + [pltpu.VMEM((2, own_rows * span, LANES), jnp.float32), pltpu.VMEM((own_rows * span, LANES), jnp.float32)]
         + [sems] * 4
-        + [pltpu.SemaphoreType.DMA((2,))],
+        + [pltpu.SemaphoreType.DMA((2,)), pltpu.SemaphoreType.DMA((1,))],
         compiler_params=pltpu.CompilerParams(
             collective_id=quads, has_side_effects=True, vmem_limit_bytes=56 * 1024 * 1024
         ),
@@ -324,8 +361,40 @@
     )(*operands)
 
 
+def distinct_tasks(lists_ref, cap, chip):
+    groups = lists_ref.shape[0]
+    span = 2 * groups
+    lane = lax.broadcasted_iota(jnp.int32, (groups, LANES), 1)
+    live = lane < jnp.minimum(lists_ref[:, 2, :], cap)
+    key = jnp.where(live, lists_ref[:, 1, :] * groups + lists_ref[:, 0, :], -1)
+    per_row = LANES // span
+    row_lane = lax.broadcasted_iota(jnp.int32, (1, LANES), 1)
+    own = jnp.zeros((1, LANES), jnp.float32)
+    most = jnp.zeros((1, 1), jnp.float32)
+    for chunk in range(groups * groups // LANES):
+        times = jnp.zeros((groups, LANES), jnp.float32)
+        for slot in range(cap):
+            times += jnp.where(key[:, slot : slot + 1] == lane + chunk * LANES, 1.0, 0.0)
+        times = jnp.sum(times, axis=0, keepdims=True)
+        for place in range(per_row):
+            inside = (row_lane >= place * span) & (row_lane < (place + 1) * span)
+            count = jnp.sum(jnp.where(inside & (times > 0.0), 1.0, 0.0), axis=1, keepdims=True)
+            most = jnp.maximum(most, count)
+            turned = pltpu.roll(times, (LANES - place * span) % LANES, 1) if place else times
+            own += jnp.where((chip == chunk * per_row + place) & (row_lane < span), turned, 0.0)
+    shape = (LANES, LANES)
+    down, across = lax.broadcasted_iota(jnp.int32, shape, 0), lax.broadcasted_iota(jnp.int32, shape, 1)
+    own_down = jnp.sum(jnp.where(down == across, own, 0.0), axis=1, keepdims=True)
+    before = jnp.sum(jnp.where((across < down) & (own > 0.0), 1.0, 0.0), axis=1, keepdims=True)
+    here = (before == across.astype(jnp.float32)) & (own_down > 0.0)
+    entry = jnp.sum(jnp.where(here, down.astype(jnp.float32), 0.0), axis=0, keepdims=True)
+    often = jnp.sum(jnp.where(here, own_down, 0.0), axis=0, keepdims=True)
+    row = lax.broadcasted_iota(jnp.int32, (8, LANES), 0)
+    return jnp.where(row == 0, entry, jnp.where(row == 1, often, most)).astype(jnp.int32)
+
+
 def gather_kernel(
-    rings, span, orbital_ref, slot_ref, pairs_ref, count_ref, window_ref, lists_ref, give, own_list,
+    rings, span, orbital_ref, slot_ref, pairs_ref, count_ref, window_ref, list_ref, lists_ref, give, own_list,
     swap_sems, list_send, list_recv, near_send, near_recv, far_send, far_recv,
 ):
     ring_x, ring_z = rings
@@ -399,51 +468,79 @@
         return lax.rem(x + ring_x, ring_x) * ring_z + lax.rem(z + ring_z, ring_z)
 
     level = (0, -1, 1, 2)
-
-    def along(ring, step):
+    later = packed // 9
+    main, rest = (1, 0, 0, packed - later), (0, 1, packed - later, later)
+    number = {main: 0, rest: 1}
+
+    def along(plan, ring, step):
+        move = [0, 0]
         if ring == 0:
-            return place(at_x, at_z + step)
-        return place(at_x + step, at_z + level[ring - 1])
-
-    def neighbour(ring, step):
-        target = place(at_x, at_z + step) if ring == 0 else place(at_x + step, at_z)
-        return 2 * target + core
-
-    def near(ring, way):
-        block = blocks(2 * along(ring, 0), 2)
-        return send(block, block, near_send.at[ring, way], near_recv.at[ring, way], neighbour(ring, 1 - 2 * way))
-
-    def far(ring, way):
-        block = blocks(2 * along(ring, -1 + 2 * way) + way, 1)
-        return send(block, block, far_send.at[ring, way], far_recv.at[ring, way], neighbour(ring, 1 - 2 * way))
-
-    def begin(ring):
+            move[plan[0]] = step
+        else:
+            move[plan[1]], move[plan[0]] = step, level[ring - 1]
+        return place(at_x + move[0], at_z + move[1])
+
+    def neighbour(plan, ring, step):
+        move = [0, 0]
+        move[plan[min(ring, 1)]] = step
+        return 2 * place(at_x + move[0], at_z + move[1]) + core
+
+    def piece(plan, chip_at, half):
+        return window_ref.at[pl.ds(pl.multiple_of((2 * chip_at + half) * packed + plan[2], 16), plan[3])]
+
+    def near(plan, ring, way, half):
+        block = piece(plan, along(plan, ring, 0), half)
+        sems = [sem.at[number[plan], ring, way, half] for sem in (near_send, near_recv)]
+        return send(block, block, *sems, neighbour(plan, ring, 1 - 2 * way))
+
+    def far(plan, ring, way):
+        block = piece(plan, along(plan, ring, -1 + 2 * way), way)
+        sems = [sem.at[number[plan], ring, way] for sem in (far_send, far_recv)]
+        return send(block, block, *sems, neighbour(plan, ring, 1 - 2 * way))
+
+    def begin_half(plan, ring, half):
         for way in range(2):
-            near(ring, way).start()
-
-    def onward(ring):
-        for way in range(2):
-            near(ring, way).wait_recv()
-            far(ring, way).start()
+            near(plan, ring, way, half).start()
+
+    def begin(plan, ring):
+        for turn in range(2):
+            for way in range(2):
+                near(plan, ring, way, way if turn == 0 else 1 - way).start()
+
+    def onward(plan, ring, way):
+        near(plan, ring, way, way).wait_recv()
+        far(plan, ring, way).start()
 
     swap(band).wait_recv()
-    begin(0)
-    begin(1)
+    begin(main, 0)
+    begin(main, 1)
+    begin(rest, 0)
     lax.fori_loop(1, groups, start_list, 0)
     for way in range(2):
-        near(0, way).wait_recv()
-        far(0, way).start()
-        begin(2 + way)
-    onward(1)
+        onward(main, 0, way)
+        begin_half(main, 2 + way, way)
     for way in range(2):
-        far(0, way).wait_recv()
-    begin(4)
-    onward(2)
-    onward(3)
-    onward(4)
-    for ring in range(1, 5):
+        onward(rest, 0, way)
+        onward(main, 1, way)
+    for way in range(2):
+        near(main, 0, way, 1 - way).wait_recv()
+        begin_half(main, 2 + way, 1 - way)
+    for way in range(2):
+        far(main, 0, way).wait_recv()
+        begin_half(main, 4, way)
+    begin(rest, 1)
+    for way in range(2):
+        near(rest, 0, way, 1 - way).wait_recv()
+        begin(rest, 2 + way)
+    for turn in range(2):
         for way in range(2):
-            far(ring, way).wait_recv()
+            onward(main, 2 + way, way if turn == 0 else 1 - way)
+    for way in range(2):
+        far(rest, 0, way).wait_recv()
+    begin(rest, 4)
+    for ring in range(1, 4):
+        for way in range(2):
+            onward(rest, ring, way)
 
     def end_list(step, carry):
         send_list(step, band).wait_recv()
@@ -452,11 +549,23 @@
 
     lax.fori_loop(1, groups, end_list, 0)
     lists_ref[band] = own_list[...]
+    list_ref[...] = distinct_tasks(lists_ref, pairs_ref.shape[1], chip)
+
+    for plan in (main, rest):
+        for way in range(2):
+            onward(plan, 4, way)
+    for plan in (main, rest):
+        for ring in range(1, 5):
+            for way in range(2):
+                near(plan, ring, way, 1 - way).wait_recv()
+                far(plan, ring, way).wait_recv()
     swap(band).wait_send()
-    for ring in range(5):
-        for way in range(2):
-            near(ring, way).wait_send()
-            far(ring, way).wait_send()
+    for plan in (main, rest):
+        for ring in range(5):
+            for way in range(2):
+                near(plan, ring, way, 0).wait_send()
+                near(plan, ring, way, 1).wait_send()
+                far(plan, ring, way).wait_send()
 
 
 def gather_window(rings, span, orbitals, window_slot, task_pairs, task_count):
@@ -469,37 +578,20 @@
         functools.partial(gather_kernel, rings, span),
         out_shape=(
             jax.ShapeDtypeStruct((groups * packed, LANES), jnp.bfloat16),
-            jax.ShapeDtypeStruct((groups, 8, LANES), jnp.int32),
+            jax.ShapeDtypeStruct((8, LANES), jnp.int32),
         ),
         in_specs=[vmem, smem, vmem, smem],
         out_specs=(vmem, vmem),
-        scratch_shapes=[pltpu.VMEM((packed, LANES), jnp.bfloat16), pltpu.VMEM((8, LANES), jnp.int32)]
+        scratch_shapes=[pltpu.VMEM((groups, 8, LANES), jnp.int32)]
+        + [pltpu.VMEM((packed, LANES), jnp.bfloat16), pltpu.VMEM((8, LANES), jnp.int32)]
         + [dma((2,)), dma((groups,)), dma((groups,))]
-        + [dma((5, 2))] * 4,
+        + [dma((2, 5, 2, 2))] * 2
+        + [dma((2, 5, 2))] * 2,
         compiler_params=pltpu.CompilerParams(
             collective_id=9, has_side_effects=True, vmem_limit_bytes=56 * 1024 * 1024
         ),
         name="gather_window",
     )(orbitals.reshape(2, slab_rows * span, span), window_slot, task_pairs[0], task_count)
-
-
-def task_lists(lists, cap, groups, group):
-    alive = jnp.arange(cap, dtype=jnp.int32)[None, :] < lists[:, 2, :1]
-    position = jnp.where(alive, lists[:, 1, :cap] * groups + lists[:, 0, :cap], -1).reshape(-1)
-    entries = jnp.arange(groups * groups, dtype=jnp.int32)
-    times = jnp.sum((position[:, None] == entries[None, :]).astype(jnp.int32), axis=0).reshape(-1, 2 * groups)
-    live = times > 0
-    most = jnp.max(jnp.sum(live.astype(jnp.int32), axis=1))
-    own_times = lax.dynamic_index_in_dim(times, group, 0, keepdims=False)
-    own_live = own_times > 0
-    local = jnp.arange(2 * groups, dtype=jnp.int32)
-    before = jnp.sum((own_live[None, :] & (local[None, :] < local[:, None])).astype(jnp.int32), axis=1)
-    here = own_live[None, :] & (before[None, :] == local[:, None])
-    entry = jnp.sum(jnp.where(here, local[None, :], 0), axis=1)
-    often = jnp.sum(jnp.where(here, own_times[None, :], 0), axis=1).astype(jnp.float32)
-    side = entry // groups
-    weights = jnp.stack([jnp.where(side == 0, often, 0.0), jnp.where(side == 1, often, 0.0)])
-    return entry % groups, 2 * group + side, weights, most
 
 
 def on_device(orbitals, exchange_in, window_slot, task_pairs, task_count):
@@ -508,26 +600,18 @@
     groups = lax.axis_size("band")
     members = 2 * grid_parts
     own_rows = span // members
-    band = lax.axis_index("band")
-    core, group = band % 2, band // 2
     window, lists = gather_window((4, 4), span, orbitals, window_slot, task_pairs, task_count)
-    sources, targets, weights, most = task_lists(lists, task_pairs.shape[-1], groups, group)
-
     window = window.reshape(groups, -1, LANES)
-    member = 2 * lax.axis_index("grid") + core
-    constants = (
-        quarter_kernel(span, member % QUAD), jnp.asarray(undo_emphasis(span)), jnp.asarray(lane_table(span)),
-        jnp.asarray(row_tables(span)),
-    )
+    constants = [jnp.asarray(a) for a in (quarter_kernels(span), undo_emphasis(span), lane_table(span), row_tables(span))]
+    most = lists[2, 0]
 
     def few():
-        return run_tasks(3, span, members, sources, targets, weights, window, *constants)
+        return run_tasks(3, span, members, jnp.zeros((1,), jnp.int32), lists, window, *constants)
 
     def many():
         def step(carry):
             start, total = carry
-            lists = [lax.dynamic_slice_in_dim(a, start, 16, a.ndim - 1) for a in (sources, targets, weights)]
-            return start + 16, total + run_tasks(4, span, members, *lists, window, *constants)
+            return start + 16, total + run_tasks(4, span, members, start[None], lists, window, *constants)
 
         zero = jnp.zeros((2, own_rows * span, LANES), jnp.float32)
         return lax.while_loop(lambda carry: carry[0] < most, step, (jnp.int32(0), zero))[1]

time: 157 us -> 107 us (0.68)
  Pallas kernels: 135 us -> 101 us
  local copies, waits for them, and re-layouts: 8.27 us -> 0.51 us
  other arithmetic: 9.78 us -> 2.62 us
    pallas_call x1, Pallas kernels: 87.1 us -> 58 us  [run_tasks(): pl.pallas_call(functools.partial(task_kernel, quads, span), out_shape=jax...]
    pallas_call x1, Pallas kernels: 48 us -> 43.1 us  [gather_window(): pl.pallas_call(functools.partial(gather_kernel, rings, span), out_shape=(...]
    dynamic_slice x4 -> x0, local copies, waits for them, and re-layouts: 2.59 us -> none  [the longest x3 1.88 us: step(): lax.dynamic_slice_in_dim(a, start, 16, a.ndim - 1)]
    add x4 -> x0, other arithmetic: 2.31 us -> none  [the longest x1 1.18 us: step(): total + run_tasks(4, span, members, *lists, window, *constants)]
where the time goes in v3:
time: 107 us; the launch traced here: 106 us
  Pallas kernels  101 us (94%)
  other arithmetic  2.62 us (2%)
  between operations  1.97 us (2%)
    pallas_call x1, Pallas kernels, run_tasks(): pl.pallas_call(functools.partial(task_kernel, quads, span), out_shape=jax...  58 us
    pallas_call x1, Pallas kernels, gather_window(): pl.pallas_call(functools.partial(gather_kernel, rings, span), out_shape=(...  43.1 us
    add x1, other arithmetic, on_device(): return exchange_in + jnp.where(slot_ids == window_slot[0], owned, 0.0)  2.62 us

profile of v3, /device:TPU:1, one launch (start us, length us, event | category | flops | bytes accessed | tf_op | source)
XLA Modules:
  0.0 106.4 jit_solution(8269045361880916924)
XLA Ops:
  1.3 43.1 %gather_window.1 = (bf16[13824,128]{1,0:T(8,128)(2,1)S(1)}, s32[8,128]{1,0:T(8,128)S(1)}) custom-call(bf16[2,1152,96]{2,1,0:T(8,128)(2,1)} %bitcast.14, s32[1]{0:T(128)} %copy.19.slot_ref, s32[2,8]{1,0:T(2,128)} %bitcast.15, s32[1]{0:T(128)S(6)} %copy.20.count_ref), custom_call_target="tpu_custom_call" | custom-call | tf_op jit(solution)/shard_map/gather_window/pallas_call | solution.py:577
  44.4 0.5 slice.6
  45.5 58.2 %conditional.1 = (f32[2,576,128]{2,1,0:T(8,128)}) conditional(s32[]{:T(128)} %convert_element_type.3, (s32[]{:T(128)}, s32[8,128]{1,0:T(8,128)S(1)}, bf16[32,432,128]{2,1,0:T(8,128)(2,1)S(1)}, f32[4,2304,128]{2,1,0:T(8,128)}, f32[96,128]{1,0:T(8,128)}, /*index=5*/bf16[256,256]{1,0:T(8,128)(2,1)}, bf16[3,192,192]{2,1,0:T(8,128)(2,1)}) %tuple.30, ...), branch_computations={%region_0.0_spmd, %region_3.0_spmd} | conditional | flops 147458 | bytes 7078153 | solution.py:619
  45.7 58.0 %exchange_tasks.2 = f32[2,576,128]{2,1,0:T(8,128)} custom-call(s32[1]{0:T(128)} %constant.12.clone.start_ref, s32[8,128]{1,0:T(8,128)S(1)} %get-tuple-element.89.list_ref, bf16[32,432,128]{2,1,0:T(8,128)(2,1)S(1)} %get-tuple-element.90.window_ref, f32[4,2304,128]{2,1,0:T(8,128)} %get-tuple-element.91.kernels_ref, f32[96,128]{1,0:T(8,128)} %get-tuple-element.92.undo_ref, ...), custom_call_target="tpu_custom_call" | custom-call | tf_op jit(solution)/shard_map/cond/branch_1_fun/exchange_tasks/pallas_call | solution.py:347
  103.7 2.6 %select_add_fusion = f32[2,12,96,96]{3,2,1,0:T(8,128)} fusion(f32[2,12,96,96]{3,2,1,0:T(8,128)} %param.14, f32[12,96,96]{2,1,0:T(8,128)} %bitcast.13, pred[2]{0:T(512)(128)(4,1)S(1)} %iota_compare_fusion), kind=kLoop, calls=%fused_computation | loop fusion | flops 442368 | bytes 2211842 | tf_op jit(solution)/shard_map/add | solution.py:622
  (1 shorter events, 0.0 us)

commit v4 on v3

--- a/solution.py
+++ b/solution.py
@@ -12,7 +12,6 @@
 MESH = pl.DeviceIdType.MESH
 LANES = 128
 QUAD = 4
-UNROLL = 3
 
 
 def hartley_table(length):
@@ -39,7 +38,7 @@
 
 def row_tables(length):
     high, low = split_table(length)
-    order = np.concatenate([np.arange(0, length, 2), np.arange(1, length, 2)])
+    order = np.arange(length).reshape(-1, 3, 2).transpose(2, 1, 0).reshape(-1)
     out = np.zeros((3, 2 * length, 2 * length), jnp.bfloat16)
     plain = np.arange(length)
     for which, pick in enumerate((np.ix_(plain, plain), np.ix_(plain, order), np.ix_(order, plain))):
@@ -103,12 +102,14 @@
     return jnp.round(values).astype(jnp.int32)
 
 
+def lanes_of(values):
+    return lax.broadcasted_iota(jnp.int32, values.shape, 1)
+
+
 def encode(first, second):
-    lane = lax.broadcasted_iota(jnp.int32, first.shape, 1)
     top = grade(jnp.max(jnp.maximum(jnp.abs(first), jnp.abs(second)), axis=(0, 1), keepdims=True))
     factor = LEVELS / size(top)
-    word = nearest(first * factor) * 65536 + nearest(second * factor)
-    return jnp.where(lane == 96, top.astype(jnp.int32), word)
+    return nearest(first * factor) * 65536 + nearest(second * factor), top.astype(jnp.int32)
 
 
 def encode_apart(first, second):
@@ -118,10 +119,8 @@
     high = grade(jnp.max(jnp.where(lane > 0, 0.0, peaks), axis=1, keepdims=True))
     factor = jnp.where(lane > 0, LEVELS / size(top), FINE / size(high))
     first, second = nearest(first * factor), nearest(second * factor)
-    lane = lax.broadcasted_iota(jnp.int32, first.shape, 1)
-    word = jnp.where(lane > 0, first * 65536 + second, first)
-    word = jnp.where(lane == 96, pltpu.roll(second, 96, 1), word)
-    return jnp.where(lane == 97, top.astype(jnp.int32), jnp.where(lane == 98, high.astype(jnp.int32), word))
+    word = jnp.where(lanes_of(first) > 0, first * 65536 + second, first)
+    return word, second, top.astype(jnp.int32), high.astype(jnp.int32)
 
 
 def halves(word):
@@ -129,25 +128,35 @@
     return lax.shift_right_arithmetic(word - second, 16), second
 
 
-def scale_of(word):
-    return size(word[:, 96:97].astype(jnp.float32)) * (1.0 / LEVELS)
-
-
 def decode(word, scale):
     return [half.astype(jnp.float32) * scale for half in halves(word)]
 
 
-def scale_apart(word):
-    lane = lax.broadcasted_iota(jnp.int32, word.shape, 1)
-    rest = size(word[:, 97:98].astype(jnp.float32)) * (1.0 / LEVELS)
-    return jnp.where(lane > 0, rest, size(word[:, 98:99].astype(jnp.float32)) * (1.0 / FINE))
-
-
-def decode_apart(word, scale):
-    lane = lax.broadcasted_iota(jnp.int32, word.shape, 1)
+def decode_apart(word, second_apart, scale):
+    lane = lanes_of(word)
     first, second = halves(word)
-    first, second = jnp.where(lane > 0, first, word), jnp.where(lane > 0, second, pltpu.roll(word, 32, 1))
+    first, second = jnp.where(lane > 0, first, word), jnp.where(lane > 0, second, second_apart)
     return [first.astype(jnp.float32) * scale, second.astype(jnp.float32) * scale]
+
+
+def beside(full, third, turn):
+    return jnp.where(lanes_of(full) < 96, full, pltpu.roll(third, turn, 1))
+
+
+def tail_lanes(pieces):
+    lane = lanes_of(pieces[0])
+    first, second = pltpu.roll(pieces[0], 64, 1), pltpu.roll(pieces[1], 96, 1)
+    return jnp.where(lane < 32, first, jnp.where(lane < 64, second, pieces[2]))
+
+
+def third_of(full, second_full, tail, group):
+    lane = lanes_of(full)
+    last = pltpu.roll(tail, 64 - 32 * group, 1) if group < 2 else tail
+    return jnp.where(lane < 32, pltpu.roll(full, 32, 1), jnp.where(lane < 64, pltpu.roll(second_full, 64, 1), last))
+
+
+def put(values, lane_at, column):
+    return jnp.where(lanes_of(values) == lane_at, column, values)
 
 
 def along_lanes(values, table):
@@ -173,7 +182,9 @@
     me = 2 * lax.axis_index("grid") + core
     own_rows = span // members
     rows = span // QUAD
-    block = own_rows // 2 * rows
+    block = 2 * rows + rows // 3
+    eighth = rows // 3
+    my_slot = me // QUAD
 
     def place(member):
         return {"band": pair + lax.rem(member, 2), "grid": member // 2}
@@ -201,22 +212,37 @@
     def local(quad, src, dst, recv_sem):
         return pltpu.make_async_copy(at(src, quad, me), at(dst, quad, me), recv_sem.at[quad, me])
 
-    def start_all(quad, src, dst, send_sem, recv_sem):
+    def start_one(quad, member, src, dst, send_sem, recv_sem):
+        @pl.when(member != me)
+        def _():
+            remote(quad, member, me, src, dst, send_sem, recv_sem).start()
+
+        @pl.when(member == me)
+        def _():
+            local(quad, src, dst, recv_sem).start()
+
+    def start_all(quad, *way):
         def step_one(step, carry):
-            remote(quad, lax.rem(me + step, members), me, src, dst, send_sem, recv_sem).start()
+            start_one(quad, lax.rem(me + step, members), *way)
             return carry
 
-        lax.fori_loop(1, members, step_one, 0)
-        local(quad, src, dst, recv_sem).start()
-
-    def wait_recv(quad, src, dst, send_sem, recv_sem):
+        lax.fori_loop(1, members + 1, step_one, 0)
+
+    def wait_one(quad, member, src, dst, send_sem, recv_sem):
+        @pl.when(member != me)
+        def _():
+            remote(quad, member, member, src, dst, send_sem, recv_sem).wait_recv()
+
+        @pl.when(member == me)
+        def _():
+            local(quad, src, dst, recv_sem).wait()
+
+    def wait_recv(quad, *way):
         def step_one(step, carry):
-            other = lax.rem(me + step, members)
-            remote(quad, other, other, src, dst, send_sem, recv_sem).wait_recv()
+            wait_one(quad, lax.rem(me + step, members), *way)
             return carry
 
-        lax.fori_loop(1, members, step_one, 0)
-        local(quad, src, dst, recv_sem).wait()
+        lax.fori_loop(1, members + 1, step_one, 0)
 
     def wait_send(quad, src, dst, send_sem, recv_sem):
         def step_one(step, carry):
@@ -241,71 +267,115 @@
         return lax.rem(entry, groups), entry // groups, list_ref[1, index].astype(jnp.float32)
 
     def inner(quad):
-        def one(slot, carry):
+        def one(step, carry):
+            slot = lax.rem(my_slot + 1 + step, QUAD)
             source, side, _ = task(quad, slot)
             target = pair + side
-            for two in range(own_rows // 2):
-                density = window_part(source, two) * window_part(target, two)
-                mixed = along_lanes(unpack(density), lane_ref[...])
-                mixed = along_rows(jnp.concatenate([mixed[:span], mixed[span:]], axis=1), row_ref[0])
-                word = encode_apart(mixed[:, :LANES], mixed[:, LANES:])
-                for quarter in range(QUAD):
-                    start = (slot * QUAD + quarter) * block + two * rows
-                    send_out[quad, pl.ds(pl.multiple_of(start, 8), rows)] = word[quarter * rows : (quarter + 1) * rows]
+            parts = range(own_rows // 2)
+            mixed = [along_lanes(unpack(window_part(source, two) * window_part(target, two)), lane_ref[...]) for two in parts]
+            mixed = [along_rows(jnp.concatenate([value[:span], value[span:]], axis=1), row_ref[0]) for value in mixed]
+            coded = [encode_apart(value[:, :LANES], value[:, LANES:]) for value in mixed]
+            words, seconds, tops, highs = zip(*coded)
+            for quarter in range(QUAD):
+                start = (slot * QUAD + quarter) * block
+                here = slice(quarter * rows, (quarter + 1) * rows)
+                third = words[2][here]
+                groups = [slice(quarter * rows + g * eighth, quarter * rows + (g + 1) * eighth) for g in range(3)]
+                tail = tail_lanes([words[2][group] for group in groups])
+                for two in parts:
+                    for g, group in enumerate(groups):
+                        at_lane = 96 + 3 * two + g
+                        tail = put(tail, at_lane, pltpu.roll(seconds[two][group], at_lane, 1))
+                    tail = put(put(tail, 105 + 2 * two, tops[two]), 106 + 2 * two, highs[two])
+                send_out[quad, pl.ds(pl.multiple_of(start, 8), rows)] = beside(words[0][here], third, 96)
+                send_out[quad, pl.ds(pl.multiple_of(start + rows, 8), rows)] = beside(words[1][here], third, 64)
+                send_out[quad, pl.ds(pl.multiple_of(start + 2 * rows, 8), eighth)] = tail
+            for quarter in range(QUAD):
+                start_one(quad, slot * QUAD + quarter, *outward)
             return carry
 
         lax.fori_loop(0, QUAD, one, 0)
 
     def outer(quad):
         wait_recv(quad, *outward)
-        scale = scale_apart(recv_out[quad, pl.ds(0, span // 2, stride=rows)])
+
+        def across(first):
+            return pl.ds(first, members, stride=block)
+
+        tail = recv_out[quad, across(2 * rows)]
+        scales = []
+        for two in range(3):
+            rest = size(tail[:, 105 + 2 * two : 106 + 2 * two].astype(jnp.float32)) * (1.0 / LEVELS)
+            mean = size(tail[:, 106 + 2 * two : 107 + 2 * two].astype(jnp.float32)) * (1.0 / FINE)
+            scales.append(jnp.where(lanes_of(tail) > 0, rest, mean))
+        scale = jnp.concatenate(scales, axis=0)
 
         def some(step, carry):
-            pairs = [step * UNROLL + i for i in range(UNROLL)]
-            picks = [[pl.ds(2 * two + half, span // 2, stride=rows) for half in range(2)] for two in pairs]
-            words = [[recv_out[quad, pick] for pick in both] for both in picks]
-            values = [
-                jnp.concatenate([jnp.concatenate(decode_apart(word, scale), axis=0) for word in both], axis=1)
-                for both in words
-            ]
+            tails = [recv_out[quad, across(2 * rows + 2 * step + half)] for half in range(2)]
+            values = []
+            for g in range(3):
+                both = []
+                for half in range(2):
+                    row = g * eighth + 2 * step + half
+                    first, second = recv_out[quad, across(row)], recv_out[quad, across(rows + row)]
+                    word = jnp.concatenate([first, second, third_of(first, second, tails[half], g)], axis=0)
+                    apart = jnp.concatenate([pltpu.roll(tails[half], 32 - 3 * two - g, 1) for two in range(3)], axis=0)
+                    both.append(jnp.concatenate(decode_apart(word, apart, scale), axis=0))
+                values.append(jnp.concatenate(both, axis=1))
             mixed = [along_rows(value, row_ref[1]) for value in values]
             factors = [
-                jnp.concatenate([kernel_ref[pl.ds(2 * two + half, span, stride=rows)] for half in range(2)], axis=1)
-                for two in pairs
+                jnp.concatenate(
+                    [kernel_ref[pl.ds(g * eighth + 2 * step + half, span, stride=rows)] for half in range(2)], axis=1
+                )
+                for g in range(3)
             ]
             restored = [along_rows(value * factor, row_ref[2]) for value, factor in zip(mixed, factors)]
-            sides = [slice(half * LANES, (half + 1) * LANES) for half in range(2)]
-            words = [[encode(value[: span // 2, side], value[span // 2 :, side]) for side in sides] for value in restored]
-            for both, pair_words in zip(picks, words):
-                for pick, word in zip(both, pair_words):
-                    send_back[quad, pick] = word
+            for half in range(2):
+                side = slice(half * LANES, (half + 1) * LANES)
+                words, tops = zip(*[encode(value[: span // 2, side], value[span // 2 :, side]) for value in restored])
+                thirds = [word[2 * members :] for word in words]
+                tail = tail_lanes(thirds)
+                for g in range(3):
+                    row = g * eighth + 2 * step + half
+                    tail = put(tail, 96 + g, tops[g])
+                    send_back[quad, across(row)] = beside(words[g][:members], thirds[g], 96)
+                    send_back[quad, across(rows + row)] = beside(words[g][members : 2 * members], thirds[g], 64)
+                send_back[quad, across(2 * rows + 2 * step + half)] = tail
             return carry
 
-        lax.fori_loop(0, rows // 2 // UNROLL, some, 0)
+        lax.fori_loop(0, eighth // 2, some, 0)
         start_all(quad, *backward)
 
     def finish(quad):
-        wait_recv(quad, *backward)
-
-        def one(slot, carry):
+        def one(step, carry):
+            slot = lax.rem(my_slot + step, QUAD)
             source, wanted, often = task(quad, slot)
             weights = [jnp.where(wanted == side, often, 0.0) for side in range(2)]
-
-            def arrived(two):
-                starts = [(slot * QUAD + quarter) * block + two * rows for quarter in range(QUAD)]
-                return jnp.concatenate(
-                    [recv_back[quad, pl.ds(pl.multiple_of(start, 8), rows)] for start in starts], axis=0
-                )
-
-            scale = scale_of(arrived(0)) * undo_ref[...]
-            for two in range(own_rows // 2):
-                mixed = decode(arrived(two), scale)
-                mixed = along_rows(jnp.concatenate(mixed, axis=1), row_ref[0])
-                potential = along_lanes(
-                    jnp.concatenate([mixed[:, :LANES], mixed[:, LANES:]], axis=0), lane_ref[...]
-                )
+            words, scales = [[], [], []], []
+            for quarter in range(QUAD):
+                wait_one(quad, slot * QUAD + quarter, *backward)
+            for quarter in range(QUAD):
+                start = (slot * QUAD + quarter) * block
+                first, second = [
+                    recv_back[quad, pl.ds(pl.multiple_of(start + two * rows, 8), rows)] for two in range(2)
+                ]
+                tail = recv_back[quad, pl.ds(pl.multiple_of(start + 2 * rows, 8), eighth)]
+                words[0].append(first)
+                words[1].append(second)
+                for g in range(3):
+                    group = slice(g * eighth, (g + 1) * eighth)
+                    words[2].append(third_of(first[group], second[group], tail, g))
+                    scales.append(tail[:, 96 + g : 97 + g])
+            scale = size(jnp.concatenate(scales, axis=0).astype(jnp.float32)) * (1.0 / LEVELS) * undo_ref[...]
+            parts = range(own_rows // 2)
+            mixed = [jnp.concatenate(decode(jnp.concatenate(words[two], axis=0), scale), axis=1) for two in parts]
+            mixed = [along_rows(value, row_ref[0]) for value in mixed]
+            potentials = [
+                along_lanes(jnp.concatenate([value[:, :LANES], value[:, LANES:]], axis=0), lane_ref[...]) for value in mixed
+            ]
+            for two in parts:
                 part = pl.ds(2 * two * span, 2 * span)
-                action = potential * unpack(window_part(source, two))
+                action = potentials[two] * unpack(window_part(source, two))
                 for side in range(2):
                     total[side, part] += action * weights[side]
             return carry
@@ -313,17 +383,14 @@
         lax.fori_loop(0, QUAD, one, 0)
 
     total[...] = jnp.zeros_like(total)
+    pl.semaphore_wait(barrier, members - 1)
     for quad in range(quads):
         inner(quad)
-        if quad == 0:
-            pl.semaphore_wait(barrier, members - 1)
-        start_all(quad, *outward)
     kernel_copy.wait()
     for quad in range(quads):
         outer(quad)
-        if quad > 0:
-            finish(quad - 1)
-    finish(quads - 1)
+    for quad in range(quads):
+        finish(quad)
 
     swap = pltpu.make_async_remote_copy(
         src_ref=total.at[1 - core], dst_ref=partner_part, send_sem=part_sems.at[0], recv_sem=part_sems.at[1],
@@ -341,7 +408,7 @@
 
 def run_tasks(quads, span, members, *operands):
     own_rows = span // members
-    whole = (quads, span * span // QUAD // 2, LANES)
+    whole = (quads, members * (span // QUAD) * 7 // 3, LANES)
     smem, vmem = pl.BlockSpec(memory_space=pltpu.SMEM), pl.BlockSpec(memory_space=pltpu.VMEM)
     sems = pltpu.SemaphoreType.DMA((quads, members))
     return pl.pallas_call(

time: 107 us -> 95.8 us (0.90)
  Pallas kernels: 101 us -> 90.3 us
    pallas_call x1, Pallas kernels: 58 us -> 47.3 us  [run_tasks(): pl.pallas_call(functools.partial(task_kernel, quads, span), out_shape=jax...]
where the time goes in v4:
time: 95.8 us; the launch traced here: 95.6 us
  Pallas kernels  90.3 us (94%)
  other arithmetic  2.62 us (3%)
  between operations  1.97 us (2%)
    pallas_call x1, Pallas kernels, run_tasks(): pl.pallas_call(functools.partial(task_kernel, quads, span), out_shape=jax...  47.3 us
    pallas_call x1, Pallas kernels, gather_window(): pl.pallas_call(functools.partial(gather_kernel, rings, span), out_shape=(...  43.1 us
    add x1, other arithmetic, on_device(): return exchange_in + jnp.where(slot_ids == window_slot[0], owned, 0.0)  2.62 us

profile of v4, /device:TPU:1, one launch (start us, length us, event | category | flops | bytes accessed | tf_op | source)
XLA Modules:
  0.0 95.6 jit_solution(11389556371015086344)
XLA Ops:
  1.3 43.1 %gather_window.1 = (bf16[13824,128]{1,0:T(8,128)(2,1)S(1)}, s32[8,128]{1,0:T(8,128)S(1)}) custom-call(bf16[2,1152,96]{2,1,0:T(8,128)(2,1)} %bitcast.14, s32[1]{0:T(128)} %copy.19.slot_ref, s32[2,8]{1,0:T(2,128)} %bitcast.15, s32[1]{0:T(128)S(6)} %copy.20.count_ref), custom_call_target="tpu_custom_call" | custom-call | tf_op jit(solution)/shard_map/gather_window/pallas_call | solution.py:644
  44.4 0.5 slice.6
  45.5 47.5 %conditional.1 = (f32[2,576,128]{2,1,0:T(8,128)}) conditional(s32[]{:T(128)} %convert_element_type.3, (s32[]{:T(128)}, s32[8,128]{1,0:T(8,128)S(1)}, bf16[32,432,128]{2,1,0:T(8,128)(2,1)S(1)}, f32[4,2304,128]{2,1,0:T(8,128)}, f32[96,128]{1,0:T(8,128)}, /*index=5*/bf16[256,256]{1,0:T(8,128)(2,1)}, bf16[3,192,192]{2,1,0:T(8,128)(2,1)}) %tuple.30, ...), branch_computations={%region_0.0_spmd, %region_3.0_spmd} | conditional | flops 147458 | bytes 7078153 | solution.py:686
  45.7 47.3 %exchange_tasks.2 = f32[2,576,128]{2,1,0:T(8,128)} custom-call(s32[1]{0:T(128)} %constant.12.clone.start_ref, s32[8,128]{1,0:T(8,128)S(1)} %get-tuple-element.89.list_ref, bf16[32,432,128]{2,1,0:T(8,128)(2,1)S(1)} %get-tuple-element.90.window_ref, f32[4,2304,128]{2,1,0:T(8,128)} %get-tuple-element.91.kernels_ref, f32[96,128]{1,0:T(8,128)} %get-tuple-element.92.undo_ref, ...), custom_call_target="tpu_custom_call" | custom-call | tf_op jit(solution)/shard_map/cond/branch_1_fun/exchange_tasks/pallas_call | solution.py:414
  93.0 2.6 %select_add_fusion = f32[2,12,96,96]{3,2,1,0:T(8,128)} fusion(f32[2,12,96,96]{3,2,1,0:T(8,128)} %param.14, f32[12,96,96]{2,1,0:T(8,128)} %bitcast.13, pred[2]{0:T(512)(128)(4,1)S(1)} %iota_compare_fusion), kind=kLoop, calls=%fused_computation | loop fusion | flops 442368 | bytes 2211842 | tf_op jit(solution)/shard_map/add | solution.py:689
  (1 shorter events, 0.0 us)

commit v5 on v4

--- a/solution.py
+++ b/solution.py
@@ -81,7 +81,7 @@
     lane = lax.broadcasted_iota(jnp.int32, (rows, LANES), 1)
     turned = [pltpu.roll(parts[third], 32 * (third + 1), 1) for third in range(3)]
     last = jnp.where(lane < 32, turned[0], jnp.where(lane < 64, turned[1], turned[2]))
-    return jnp.concatenate([jnp.where(lane < 96, part, 0.0) for part in (*parts, last)], axis=0)
+    return jnp.concatenate([*parts, last], axis=0)
 
 
 LEVELS = 32766.0
@@ -109,7 +109,7 @@
 def encode(first, second):
     top = grade(jnp.max(jnp.maximum(jnp.abs(first), jnp.abs(second)), axis=(0, 1), keepdims=True))
     factor = LEVELS / size(top)
-    return nearest(first * factor) * 65536 + nearest(second * factor), top.astype(jnp.int32)
+    return lax.shift_left(nearest(first * factor), 16) + nearest(second * factor), top.astype(jnp.int32)
 
 
 def encode_apart(first, second):
@@ -119,7 +119,7 @@
     high = grade(jnp.max(jnp.where(lane > 0, 0.0, peaks), axis=1, keepdims=True))
     factor = jnp.where(lane > 0, LEVELS / size(top), FINE / size(high))
     first, second = nearest(first * factor), nearest(second * factor)
-    word = jnp.where(lanes_of(first) > 0, first * 65536 + second, first)
+    word = jnp.where(lanes_of(first) > 0, lax.shift_left(first, 16) + second, first)
     return word, second, top.astype(jnp.int32), high.astype(jnp.int32)
 
 
@@ -457,11 +457,11 @@
     entry = jnp.sum(jnp.where(here, down.astype(jnp.float32), 0.0), axis=0, keepdims=True)
     often = jnp.sum(jnp.where(here, own_down, 0.0), axis=0, keepdims=True)
     row = lax.broadcasted_iota(jnp.int32, (8, LANES), 0)
-    return jnp.where(row == 0, entry, jnp.where(row == 1, often, most)).astype(jnp.int32)
+    return jnp.where(row == 0, entry, often).astype(jnp.int32), most
 
 
 def gather_kernel(
-    rings, span, orbital_ref, slot_ref, pairs_ref, count_ref, window_ref, list_ref, lists_ref, give, own_list,
+    rings, span, orbital_ref, slot_ref, pairs_ref, count_ref, window_ref, list_ref, most_ref, lists_ref, give, own_list,
     swap_sems, list_send, list_recv, near_send, near_recv, far_send, far_recv,
 ):
     ring_x, ring_z = rings
@@ -578,9 +578,11 @@
         near(plan, ring, way, way).wait_recv()
         far(plan, ring, way).start()
 
+    for ring in range(2):
+        begin_half(main, ring, core)
     swap(band).wait_recv()
-    begin(main, 0)
-    begin(main, 1)
+    for ring in range(2):
+        begin_half(main, ring, 1 - core)
     begin(rest, 0)
     lax.fori_loop(1, groups, start_list, 0)
     for way in range(2):
@@ -616,7 +618,8 @@
 
     lax.fori_loop(1, groups, end_list, 0)
     lists_ref[band] = own_list[...]
-    list_ref[...] = distinct_tasks(lists_ref, pairs_ref.shape[1], chip)
+    list_ref[...], most = distinct_tasks(lists_ref, pairs_ref.shape[1], chip)
+    most_ref[0] = jnp.max(most).astype(jnp.int32)
 
     for plan in (main, rest):
         for way in range(2):
@@ -646,9 +649,10 @@
         out_shape=(
             jax.ShapeDtypeStruct((groups * packed, LANES), jnp.bfloat16),
             jax.ShapeDtypeStruct((8, LANES), jnp.int32),
+            jax.ShapeDtypeStruct((1,), jnp.int32),
         ),
         in_specs=[vmem, smem, vmem, smem],
-        out_specs=(vmem, vmem),
+        out_specs=(vmem, vmem, smem),
         scratch_shapes=[pltpu.VMEM((groups, 8, LANES), jnp.int32)]
         + [pltpu.VMEM((packed, LANES), jnp.bfloat16), pltpu.VMEM((8, LANES), jnp.int32)]
         + [dma((2,)), dma((groups,)), dma((groups,))]
@@ -667,10 +671,10 @@
     groups = lax.axis_size("band")
     members = 2 * grid_parts
     own_rows = span // members
-    window, lists = gather_window((4, 4), span, orbitals, window_slot, task_pairs, task_count)
+    window, lists, most = gather_window((4, 4), span, orbitals, window_slot, task_pairs, task_count)
     window = window.reshape(groups, -1, LANES)
     constants = [jnp.asarray(a) for a in (quarter_kernels(span), undo_emphasis(span), lane_table(span), row_tables(span))]
-    most = lists[2, 0]
+    most = most[0]
 
     def few():
         return run_tasks(3, span, members, jnp.zeros((1,), jnp.int32), lists, window, *constants)

time: 95.8 us -> 112 us (1.17)
  Pallas kernels: 90.3 us -> 103 us
  loops' own time: 0.2 us -> 1.63 us
  other arithmetic: 2.62 us -> 3.8 us
  local copies, waits for them, and re-layouts: 0.51 us -> 1.68 us
    pallas_call x1, Pallas kernels: 47.3 us -> 62.4 us  [run_tasks(): pl.pallas_call(functools.partial(task_kernel, quads, span), out_shape=jax...]
    pallas_call x1, Pallas kernels: 43.1 us -> 40.7 us  [gather_window(): pl.pallas_call(functools.partial(gather_kernel, rings, span), out_shape=(...]
    another operation x0 -> x1, loops' own time: none -> 1.43 us  [many(): lax.while_loop(lambda carry: carry[0] < most, step, (jnp.int32(0), zero))[1]]
    add x0 -> x1, other arithmetic: none -> 1.18 us  [step(): total + run_tasks(4, span, members, start[None], lists, window, *constants)]
where the time goes in v5:
time: 112 us
  Pallas kernels  103 us (92%)
  other arithmetic  3.8 us (3%)
  between operations  2.01 us (2%)
  local copies, waits for them, and re-layouts  1.68 us (2%)
  loops' own time  1.63 us (1%)
    pallas_call x1, Pallas kernels, run_tasks(): pl.pallas_call(functools.partial(task_kernel, quads, span), out_shape=jax...  62.4 us
    pallas_call x1, Pallas kernels, gather_window(): pl.pallas_call(functools.partial(gather_kernel, rings, span), out_shape=(...  40.7 us
    add x1, other arithmetic, on_device(): return exchange_in + jnp.where(slot_ids == window_slot[0], owned, 0.0)  2.62 us

profile of v5, /device:TPU:1, one launch (start us, length us, event | category | flops | bytes accessed | tf_op | source)
XLA Modules:
  0.0 112.2 jit_solution(9134328638742571563)
XLA Ops:
  1.3 40.7 %gather_window.1 = (bf16[13824,128]{1,0:T(8,128)(2,1)S(1)}, s32[8,128]{1,0:T(8,128)S(1)}, s32[1]{0:T(128)}) custom-call(bf16[2,1152,96]{2,1,0:T(8,128)(2,1)} %bitcast.14, s32[1]{0:T(128)} %copy.19.slot_ref, s32[2,8]{1,0:T(2,128)} %bitcast.15, s32[1]{0:T(128)S(6)} %copy.20.count_ref), custom_call_target="tpu_custom_call" | custom-call | tf_op jit(solution)/shard_map/gather_window/pallas_call | solution.py:647
  42.7 66.9 %conditional.1 = (f32[2,576,128]{2,1,0:T(8,128)}) conditional(s32[]{:T(128)} %convert_element_type.3, (s32[]{:T(128)}, s32[8,128]{1,0:T(8,128)S(1)}, bf16[32,432,128]{2,1,0:T(8,128)(2,1)S(1)}, f32[4,2304,128]{2,1,0:T(8,128)}, f32[96,128]{1,0:T(8,128)}, /*index=5*/bf16[256,256]{1,0:T(8,128)(2,1)}, bf16[3,192,192]{2,1,0:T(8,128)(2,1)}) %tuple.30, ...), branch_computations={%region_0.0_spmd, %region_3.0_spmd} | conditional | flops 147458 | bytes 7078153 | solution.py:690
  42.7 0.9 broadcast.7
  43.5 65.8 %while.9 = (s32[]{:T(128)}, f32[2,576,128]{2,1,0:T(8,128)}, s32[]{:T(128)}, s32[8,128]{1,0:T(8,128)S(1)}, bf16[32,432,128]{2,1,0:T(8,128)(2,1)S(1)}, /*index=5*/...) while((s32[]{:T(128)}, f32[2,576,128]{2,1,0:T(8,128)}, ...), condition=%wide.region_2.0_spmd, body=%wide.region_1.0_spmd.sunk | while | flops 147458 | bytes 6488229 | solution.py:688
  44.2 0.0 copy-start
  44.3 62.4 %exchange_tasks.3 = f32[2,576,128]{2,1,0:T(8,128)} custom-call(s32[1]{0:T(128)} %bitcast.9.start_ref, s32[8,128]{1,0:T(8,128)S(1)} %get-tuple-element.198.list_ref, bf16[32,432,128]{2,1,0:T(8,128)(2,1)S(1)} %get-tuple-element.199.window_ref, f32[4,2304,128]{2,1,0:T(8,128)} %get-tuple-element.200.kernels_ref, f32[96,128]{1,0:T(8,128)} %get-tuple-element.201.undo_ref, ...), custom_call_target="tpu_custom_call" | custom-call | tf_op jit(solution)/shard_map/cond/branch_0_fun/while/body/exchange_tasks/pallas_call | solution.py:414
  106.7 0.0 copy-done
  106.7 1.2 %add.14 = f32[2,576,128]{2,1,0:T(8,128)S(1)} add(f32[2,576,128]{2,1,0:T(8,128)S(1)} %copy-done, f32[2,576,128]{2,1,0:T(8,128)} %exchange_tasks.3) | non-fusion elementwise | flops 147456 | bytes 1769472 | tf_op jit(solution)/shard_map/cond/branch_0_fun/while/body/add | solution.py:685
  107.9 0.0 copy-start.1
  107.9 0.8 copy-done.1
  109.6 2.6 %select_add_fusion = f32[2,12,96,96]{3,2,1,0:T(8,128)} fusion(f32[2,12,96,96]{3,2,1,0:T(8,128)} %param.14, f32[12,96,96]{2,1,0:T(8,128)} %bitcast.13, pred[2]{0:T(512)(128)(4,1)S(1)} %iota_compare_fusion), kind=kLoop, calls=%fused_computation | loop fusion | flops 442368 | bytes 2211842 | tf_op jit(solution)/shard_map/add | solution.py:693
  (1 shorter events, 0.0 us)
Async XLA Ops:
  44.2 62.4 %copy-start = (f32[2,576,128]{2,1,0:T(8,128)S(1)}, f32[2,576,128]{2,1,0:T(8,128)}, u32[]{:S(2)}) copy-start(f32[2,576,128]{2,1,0:T(8,128)} %get-tuple-element.186) | copy-start | bytes 1769476 | tf_op jit(solution)/shard_map/cond/branch_0_fun/while
  107.9 0.8 copy-start.1

commit v6 on v4

--- a/solution.py
+++ b/solution.py
@@ -81,7 +81,7 @@
     lane = lax.broadcasted_iota(jnp.int32, (rows, LANES), 1)
     turned = [pltpu.roll(parts[third], 32 * (third + 1), 1) for third in range(3)]
     last = jnp.where(lane < 32, turned[0], jnp.where(lane < 64, turned[1], turned[2]))
-    return jnp.concatenate([jnp.where(lane < 96, part, 0.0) for part in (*parts, last)], axis=0)
+    return jnp.concatenate([*parts, last], axis=0)
 
 
 LEVELS = 32766.0
@@ -109,7 +109,7 @@
 def encode(first, second):
     top = grade(jnp.max(jnp.maximum(jnp.abs(first), jnp.abs(second)), axis=(0, 1), keepdims=True))
     factor = LEVELS / size(top)
-    return nearest(first * factor) * 65536 + nearest(second * factor), top.astype(jnp.int32)
+    return lax.shift_left(nearest(first * factor), 16) + nearest(second * factor), top.astype(jnp.int32)
 
 
 def encode_apart(first, second):
@@ -119,7 +119,7 @@
     high = grade(jnp.max(jnp.where(lane > 0, 0.0, peaks), axis=1, keepdims=True))
     factor = jnp.where(lane > 0, LEVELS / size(top), FINE / size(high))
     first, second = nearest(first * factor), nearest(second * factor)
-    word = jnp.where(lanes_of(first) > 0, first * 65536 + second, first)
+    word = jnp.where(lanes_of(first) > 0, lax.shift_left(first, 16) + second, first)
     return word, second, top.astype(jnp.int32), high.astype(jnp.int32)
 
 

time: 95.8 us -> 95.8 us (level)
  no operation moved by 1% of the time
where the time goes in v6:
time: 95.8 us; the launch traced here: 95.6 us
  Pallas kernels  90.3 us (94%)
  other arithmetic  2.62 us (3%)
  between operations  1.97 us (2%)
    pallas_call x1, Pallas kernels, run_tasks(): pl.pallas_call(functools.partial(task_kernel, quads, span), out_shape=jax...  47.3 us
    pallas_call x1, Pallas kernels, gather_window(): pl.pallas_call(functools.partial(gather_kernel, rings, span), out_shape=(...  43.1 us
    add x1, other arithmetic, on_device(): return exchange_in + jnp.where(slot_ids == window_slot[0], owned, 0.0)  2.62 us

profile of v6, /device:TPU:1, one launch (start us, length us, event | category | flops | bytes accessed | tf_op | source)
XLA Modules:
  0.0 95.6 jit_solution(2416156066538698643)
XLA Ops:
  1.3 43.1 %gather_window.1 = (bf16[13824,128]{1,0:T(8,128)(2,1)S(1)}, s32[8,128]{1,0:T(8,128)S(1)}) custom-call(bf16[2,1152,96]{2,1,0:T(8,128)(2,1)} %bitcast.14, s32[1]{0:T(128)} %copy.19.slot_ref, s32[2,8]{1,0:T(2,128)} %bitcast.15, s32[1]{0:T(128)S(6)} %copy.20.count_ref), custom_call_target="tpu_custom_call" | custom-call | tf_op jit(solution)/shard_map/gather_window/pallas_call | solution.py:644
  44.4 0.5 slice.6
  45.5 47.5 %conditional.1 = (f32[2,576,128]{2,1,0:T(8,128)}) conditional(s32[]{:T(128)} %convert_element_type.3, (s32[]{:T(128)}, s32[8,128]{1,0:T(8,128)S(1)}, bf16[32,432,128]{2,1,0:T(8,128)(2,1)S(1)}, f32[4,2304,128]{2,1,0:T(8,128)}, f32[96,128]{1,0:T(8,128)}, /*index=5*/bf16[256,256]{1,0:T(8,128)(2,1)}, bf16[3,192,192]{2,1,0:T(8,128)(2,1)}) %tuple.30, ...), branch_computations={%region_0.0_spmd, %region_3.0_spmd} | conditional | flops 147458 | bytes 7078153 | solution.py:686
  45.7 47.3 %exchange_tasks.2 = f32[2,576,128]{2,1,0:T(8,128)} custom-call(s32[1]{0:T(128)} %constant.12.clone.start_ref, s32[8,128]{1,0:T(8,128)S(1)} %get-tuple-element.89.list_ref, bf16[32,432,128]{2,1,0:T(8,128)(2,1)S(1)} %get-tuple-element.90.window_ref, f32[4,2304,128]{2,1,0:T(8,128)} %get-tuple-element.91.kernels_ref, f32[96,128]{1,0:T(8,128)} %get-tuple-element.92.undo_ref, ...), custom_call_target="tpu_custom_call" | custom-call | tf_op jit(solution)/shard_map/cond/branch_1_fun/exchange_tasks/pallas_call | solution.py:414
  93.0 2.6 %select_add_fusion = f32[2,12,96,96]{3,2,1,0:T(8,128)} fusion(f32[2,12,96,96]{3,2,1,0:T(8,128)} %param.14, f32[12,96,96]{2,1,0:T(8,128)} %bitcast.13, pred[2]{0:T(512)(128)(4,1)S(1)} %iota_compare_fusion), kind=kLoop, calls=%fused_computation | loop fusion | flops 442368 | bytes 2211842 | tf_op jit(solution)/shard_map/add | solution.py:689
  (1 shorter events, 0.0 us)
